TPU v7x, 32 devices: a whole 2x2x4 slice. The times are simulated.
32 devices in a mesh: member: 2 (over x), tile: 16 (over z, y, core).
Axes of the slice: x: 2, y: 2, z: 4, core: 2. Of those that a mesh axis runs over, the one named last changes fastest.
Arguments:
- noise_seeds: int32 [4], P('member'), parts along dimension 0, may hold values from 0 to 2147483646
- diffusivity: float32 [128, 256], P('tile'), may hold values from 0.03 to 0.24
- wet_mask: int32 [128, 256], P('tile'), may hold values 0 or 1
- vert_factor: float32 [75, 75], replicated, may hold values from -0.75 to 0.75
- norm_scale: float32 [128, 256], P('tile'), may hold values from 0.5 to 8
- obs_cell: int32 [16, 16, 128], P('tile'), may hold values from 0 to 2046, as said below
- obs_frac: float32 [16, 16, 2, 128], P('tile'), may hold values from 0 to 1
- obs_count: int32 [16, 16], P('tile'), may hold values from 32 to 128, as said below
Outputs:
- perturbation: bfloat16 [150, 128, 256], P('member', 'tile'), parts along dimension 0
- profiles: bfloat16 [16, 16, 150, 128], P('tile', None, 'member'), parts along dimension 2
There are 2 independent parts, one for each index of `member`. A program takes and returns all parts, laid end to end along the dimension named above; an argument that names none is the same for every part. Nothing has to cross between parts.
Inputs may be any that keep to these rules, and one draw needn't show every extreme that they name: `obs_cell`: each entry is row * 256 + column of an anchor cell in the owner tile's block of 8 x 256 cells, with column below 255, and row below 7 where the owner is the last tile. `obs_count`: some owner receives 128 live slots from every holder, and other counts vary by owner.
All inputs are finite; a program needn't handle non-finite values. No bound on the sum of `wet_mask` on one device may be relied on, other than what follows from the above.
Results may differ from a plain program's by a relative error of at most 0.0045.
Values may be sent and summed in bfloat16 or wider, within the bound.
A program may use at most 64 MiB of HBM per device.

v0:
```python
import jax
import jax.numpy as jnp
from jax import lax
from jax.sharding import PartitionSpec as P

STEPS = 8


def extended(block, sides, width):
    for axis, dim in sides:
        count = lax.axis_size(axis)
        forward = [(i, i + 1) for i in range(count - 1)]
        backward = [(target, source) for source, target in forward]
        low = lax.ppermute(
            lax.slice_in_dim(block, block.shape[dim] - width, None, axis=dim), axis, forward
        )
        high = lax.ppermute(lax.slice_in_dim(block, 0, width, axis=dim), axis, backward)
        block = jnp.concatenate([low, block, high], axis=dim)
    return block


def from_behind(shard, axis, by):
    count = lax.axis_size(axis)
    pairs = [(i, i + by) for i in range(count) if 0 <= i + by < count]
    return lax.ppermute(shard, axis, pairs)


def scramble(hashed):
    hashed = jnp.bitwise_xor(hashed, hashed >> 16 & 65535) * -2048144789
    hashed = jnp.bitwise_xor(hashed, hashed >> 13 & 524287) * -1028477387
    return jnp.bitwise_xor(hashed, hashed >> 16 & 65535)


def cell_noise(noise_seeds, counter):
    hashed = scramble(counter * -1640531535 + noise_seeds[0])
    hashed = scramble(jnp.bitwise_xor(hashed, noise_seeds[1]))
    uniform = ((hashed >> 8 & 16777215).astype(jnp.float32) + 0.5) * (1.0 / 16777216.0)
    return (uniform - 0.5) * 3.4641016151377544


def face_terms(wet_pad):
    face_rows = jnp.sqrt(wet_pad[1:] * wet_pad[:-1])
    face_cols = jnp.sqrt(wet_pad[:, 1:] * wet_pad[:, :-1])
    return (face_rows, face_cols)


def diffuse(padded, face_rows, face_cols):
    flux_rows = face_rows[None] * (padded[:, 1:] - padded[:, :-1])
    flux_cols = face_cols[None] * (padded[:, :, 1:] - padded[:, :, :-1])
    zero_col = jnp.zeros(flux_cols.shape[:2] + (1,), jnp.float32)
    net_cols = jnp.concatenate([flux_cols, zero_col], 2) - jnp.concatenate([zero_col, flux_cols], 2)
    return padded[:, 1:-1] + (flux_rows[:, 1:] - flux_rows[:, :-1]) + net_cols[:, 1:-1]


def bilinear(flat_field, anchor, frac_y, frac_x, columns):
    corner_nw = jnp.take(flat_field, anchor, axis=1).astype(jnp.float32)
    corner_ne = jnp.take(flat_field, anchor + 1, axis=1).astype(jnp.float32)
    corner_sw = jnp.take(flat_field, anchor + columns, axis=1).astype(jnp.float32)
    corner_se = jnp.take(flat_field, anchor + columns + 1, axis=1).astype(jnp.float32)
    blended = (1.0 - frac_y) * ((1.0 - frac_x) * corner_nw + frac_x * corner_ne) + frac_y * (
        (1.0 - frac_x) * corner_sw + frac_x * corner_se
    )
    return blended


def answer_probes(flat_field, arrived, columns):
    anchor = arrived[:, 0, 0, :].astype(jnp.int32)
    blended = bilinear(flat_field, anchor, arrived[:, 0, 1, :], arrived[:, 0, 2, :], columns)
    return jnp.transpose(blended, (1, 0, 2))[:, None].astype(jnp.bfloat16)


def noise_rows(noise_seeds, levels, row_count, first_row, total_rows, columns, wet_rows):
    shape_all = (levels, row_count, columns)
    level_ids = lax.broadcasted_iota(jnp.int32, shape_all, 0)
    row_ids = lax.broadcasted_iota(jnp.int32, shape_all, 1) + first_row
    col_ids = lax.broadcasted_iota(jnp.int32, shape_all, 2)
    counter = (level_ids * total_rows + row_ids) * columns + col_ids
    return cell_noise(noise_seeds, counter) * wet_rows[None]


def sweep(padded, face_rows, face_cols, halo_depth, tile_rows):
    for inner_step in range(halo_depth):
        reach = halo_depth - inner_step
        padded = diffuse(
            padded,
            face_rows[inner_step : inner_step + tile_rows + 2 * reach - 1],
            face_cols[inner_step : inner_step + tile_rows + 2 * reach],
        )
    return padded


def body(
    noise_seeds, diffusivity, wet_mask, vert_factor, norm_scale, obs_cell, obs_frac, obs_count
):
    tile_rows, columns = diffusivity.shape
    levels = vert_factor.shape[0]
    total_rows = tile_rows * lax.axis_size("tile")
    probes = jnp.concatenate([obs_cell.astype(jnp.float32)[:, :, None, :], obs_frac], 2)
    halo_depth = STEPS
    wet_float = wet_mask.astype(jnp.float32)
    wet_kappa = diffusivity * wet_float
    wet_pad = extended(wet_kappa, (("tile", 0),), halo_depth)
    face_rows, face_cols = face_terms(wet_pad)
    first_row = lax.axis_index("tile") * tile_rows
    wet_rows = (wet_pad > 0.0).astype(jnp.float32)
    padded = noise_rows(
        noise_seeds,
        levels,
        tile_rows + 2 * halo_depth,
        first_row - halo_depth,
        total_rows,
        columns,
        wet_rows,
    )
    state_field = sweep(padded, face_rows, face_cols, halo_depth, tile_rows)
    shape_all = (levels, tile_rows, columns)
    mixed_levels = jnp.dot(
        vert_factor,
        state_field.reshape(levels, tile_rows * columns),
        precision=lax.Precision.HIGHEST,
        preferred_element_type=jnp.float32,
    )
    perturbation = (mixed_levels.reshape(shape_all) * norm_scale[None]).astype(jnp.bfloat16)
    below_row = from_behind(perturbation[:, :1], "tile", -1)
    flat_field = jnp.concatenate([perturbation, below_row], 1).reshape(
        levels, (tile_rows + 1) * columns
    )
    result = lax.all_to_all(
        answer_probes(
            flat_field,
            lax.all_to_all(probes, "tile", split_axis=1, concat_axis=0, tiled=True),
            columns,
        ),
        "tile",
        split_axis=0,
        concat_axis=1,
        tiled=True,
    )
    slot_ids = jnp.arange(result.shape[3], dtype=jnp.int32)
    live_slot = slot_ids[None, None, None, :] < obs_count[:, :, None, None]
    profiles = jnp.where(live_slot, result, jnp.zeros_like(result))
    return (perturbation, profiles)


def solution(mesh):
    in_specs = (
        P("member"),
        P("tile", None),
        P("tile", None),
        P(),
        P("tile", None),
        P("tile", None, None),
        P("tile", None, None, None),
        P("tile", None),
    )
    out_specs = (P("member", "tile", None), P("tile", None, "member", None))
    return jax.shard_map(body, mesh=mesh, in_specs=in_specs, out_specs=out_specs, check_vma=False)
```

profile of v0, /device:TPU:0, one launch (start us, length us, event | category | flops | bytes accessed | tf_op | source)
XLA Modules:
  0.0 87.3 jit_solution(14176584301633445498)
XLA Ops:
  0.6 0.7 convert_multiply_fusion
  1.4 2.3 %collective-permute-start = (f32[8,256]{1,0:T(8,128)S(1)}, f32[8,256]{1,0:T(8,128)S(1)}, u32[]{:S(2)}, u32[]{:S(2)}) collective-permute-start(f32[8,256]{1,0:T(8,128)S(1)} %convert_multiply_fusion), channel_id=1, source_target_pairs={{0,1},{1,2},{2,3},{3,4},{4,5},{5,6},{6,7},{7,8},{8,9},{9,10},{10,1... | collective-permute-start | bytes 24584 | tf_op jit(solution)/shard_map/ppermute | solution.py:14
  3.7 1.3 %collective-permute-start.1 = (f32[8,256]{1,0:T(8,128)S(1)}, f32[8,256]{1,0:T(8,128)S(1)}, u32[]{:S(2)}, u32[]{:S(2)}) collective-permute-start(f32[8,256]{1,0:T(8,128)S(1)} %convert_multiply_fusion), channel_id=1, source_target_pairs={{1,0},{2,1},{3,2},{4,3},{5,4},{6,5},{7,6},{8,7},{9,8},{10,9},{11,1... | collective-permute-start | bytes 24584 | tf_op jit(solution)/shard_map/ppermute | solution.py:17
  5.7 1.3 %pad_maximum_fusion.1 = f32[1,16,3,128]{3,2,0,1:T(4,128)} fusion(f32[1,16,2,128]{3,2,0,1:T(2,128)} %bitcast.75, f32[1,16,1,128]{3,2,0,1:T(1,128)S(1)} %bitcast.74), kind=kLoop, calls=%fused_computation.75 | loop fusion | flops 6144 | bytes 49152 | tf_op jit(solution)/shard_map/concatenate | solution.py:98
  7.1 9.3 %all-to-all-start = ((f32[1,16,3,128]{3,2,0,1:T(4,128)}), f32[1,16,3,128]{3,2,0,1:T(4,128)S(1)}, u32[]{:S(2)}, u32[]{:S(2)}) async-start(f32[1,16,3,128]{3,2,0,1:T(4,128)} %pad_maximum_fusion.1), calls=%async_computation | async-start | bytes 65536 | tf_op jit(solution)/shard_map/all_to_all | solution.py:131
  16.4 1.3 %fusion.37 = (s32[1]{0:T(128)}, s32[1]{0:T(128)}) fusion(s32[2]{0:T(128)} %param.10), kind=kLoop, calls=%fused_computation.102 | loop fusion | bytes 16 | tf_op jit(solution)/shard_map/slice | solution.py:35
  17.9 3.1 %add_multiply_fusion = f32[75,24,256]{2,1,0:T(8,128)S(1)} fusion(f32[24,256]{1,0:T(8,128)S(1)} %get-tuple-element.9, s32[]{:T(128)} %bitcast.1, s32[]{:T(128)} %bitcast, s32[24]{0:T(128)S(1)} %iota_add_fusion, s32[75]{0:T(128)S(1)} %iota_multiply_fusion), kind=kLoop, calls=%fused_computation.32 | loop fusion | flops 16128000 | bytes 1868180 | tf_op jit(solution)/shard_map/mul | solution.py:78
  22.1 1.4 %fusion.10 = f32[75,22,256]{2,1,0:T(8,128)S(1)} fusion(f32[75,24,255]{2,1,0:T(8,128)S(1)} %fusion.11, f32[75,23,256]{2,1,0:T(8,128)S(1)} %fusion.13, f32[75,24,256]{2,1,0:T(8,128)S(1)} %add_multiply_fusion), kind=kLoop, calls=%fused_computation.25 | loop fusion | flops 1689600 | bytes 8594400 | tf_op jit(solution)/shard_map/add | solution.py:52
  24.3 1.3 %fusion.6 = f32[75,20,256]{2,1,0:T(8,128)S(1)} fusion(f32[75,22,255]{2,1,0:T(8,128)S(1)} %fusion.7, f32[75,21,256]{2,1,0:T(8,128)S(1)} %fusion.9, f32[75,22,256]{2,1,0:T(8,128)S(1)} %fusion.10), kind=kLoop, calls=%fused_computation.17 | loop fusion | flops 1536000 | bytes 7827000 | tf_op jit(solution)/shard_map/add | solution.py:52
  26.4 1.4 %fusion.2 = f32[75,18,256]{2,1,0:T(8,128)S(1)} fusion(f32[75,20,255]{2,1,0:T(8,128)S(1)} %fusion.3, f32[75,19,256]{2,1,0:T(8,128)S(1)} %fusion.5, f32[75,20,256]{2,1,0:T(8,128)S(1)} %fusion.6), kind=kLoop, calls=%fused_computation.9 | loop fusion | flops 1382400 | bytes 7059600 | tf_op jit(solution)/shard_map/add | solution.py:52
  28.6 0.9 %fusion.28 = f32[75,16,256]{2,1,0:T(8,128)S(1)} fusion(f32[75,18,255]{2,1,0:T(8,128)S(1)} %fusion, f32[75,17,256]{2,1,0:T(8,128)S(1)} %fusion.1, f32[75,18,256]{2,1,0:T(8,128)S(1)} %fusion.2), kind=kLoop, calls=%fused_computation.62 | loop fusion | flops 1228800 | bytes 6292200 | tf_op jit(solution)/shard_map/add | solution.py:52
  30.1 0.8 fusion.24
  31.5 0.9 %fusion.20 = f32[75,12,256]{2,1,0:T(8,128)S(1)} fusion(f32[75,14,255]{2,1,0:T(8,128)S(1)} %fusion.21, f32[75,13,256]{2,1,0:T(8,128)S(1)} %fusion.23, f32[75,14,256]{2,1,0:T(8,128)S(1)} %fusion.24), kind=kLoop, calls=%fused_computation.46 | loop fusion | flops 921600 | bytes 4757400 | tf_op jit(solution)/shard_map/add | solution.py:52
  33.0 0.7 fusion.16
  36.1 1.3 %collective-permute-start.2 = (bf16[75,1,256]{2,1,0:T(2,128)(2,1)S(1)}, bf16[75,1,256]{2,1,0:T(2,128)(2,1)S(1)}, u32[]{:S(2)}, u32[]{:S(2)}) collective-permute-start(bf16[75,1,256]{2,1,0:T(2,128)(2,1)S(1)} %slice.437), channel_id=1, source_target_pairs={{1,0},{2,1},{3,2},{4,3},{5,4},{6,5},{7,6},{8,7},{9,8},{10,9},{11,1... | collective-permute-start | bytes 115208 | tf_op jit(solution)/shard_map/ppermute | solution.py:25
  37.5 1.8 %collective-permute-done.2 = bf16[75,1,256]{2,1,0:T(2,128)(2,1)S(1)} collective-permute-done((bf16[75,1,256]{2,1,0:T(2,128)(2,1)S(1)}, bf16[75,1,256]{2,1,0:T(2,128)(2,1)S(1)}, u32[]{:S(2)}, u32[]{:S(2)}) %collective-permute-start.2) | collective-permute-done | bytes 38432 | tf_op jit(solution)/shard_map/ppermute | solution.py:25
  39.9 6.2 %gather_fusion = bf16[2048,75]{1,0:T(8,128)(2,1)S(1)} fusion(bf16[75,2304]{0,1:T(8,128)(2,1)S(1)} %bitcast.55, s32[2048]{0:T(1024)S(1)} %get-tuple-element.14), kind=kCustom, calls=%fused_computation.clone | custom fusion | bytes 622592 | tf_op jit(solution)/shard_map/jit(_take)/gather | solution.py:56
  46.4 6.2 %gather_fusion.1 = bf16[2048,75]{1,0:T(8,128)(2,1)S(1)} fusion(bf16[75,2304]{0,1:T(8,128)(2,1)S(1)} %bitcast.56, s32[2048]{0:T(1024)S(1)} %get-tuple-element.15), kind=kCustom, calls=%fused_computation.1.clone | custom fusion | bytes 622592 | tf_op jit(solution)/shard_map/jit(_take)/gather | solution.py:57
  52.8 6.2 %gather_fusion.2 = bf16[2048,75]{1,0:T(8,128)(2,1)S(1)} fusion(bf16[75,2304]{0,1:T(8,128)(2,1)S(1)} %bitcast.57, s32[2048]{0:T(1024)S(1)} %get-tuple-element.16), kind=kCustom, calls=%fused_computation.2.clone | custom fusion | bytes 622592 | tf_op jit(solution)/shard_map/jit(_take)/gather | solution.py:58
  59.3 6.2 %gather_fusion.3 = bf16[2048,75]{1,0:T(8,128)(2,1)S(1)} fusion(bf16[75,2304]{0,1:T(8,128)(2,1)S(1)} %bitcast.58, s32[2048]{0:T(1024)S(1)} %get-tuple-element.17), kind=kCustom, calls=%fused_computation.3.clone | custom fusion | bytes 622592 | tf_op jit(solution)/shard_map/jit(_take)/gather | solution.py:59
  65.8 1.3 %fusion.33 = bf16[16,1,75,128]{3,2,1,0:T(8,128)(2,1)} fusion(bf16[16,128,75]{1,2,0:T(8,128)(2,1)S(1)} %copy.22, bf16[16,128,75]{1,2,0:T(8,128)(2,1)S(1)} %copy.21, f32[16,128]{1,0:T(8,128)S(1)} %bitcast.71, bf16[16,128,75]{1,2,0:T(8,128)(2,1)S(1)} %copy.20, f32[16,128]{1,0:T(8,128)S(1)} %bitcast.69, bf16[16,128,75]{1,2,0:T(8,128)(2,1)S(1)} %copy.19, ...), kind=kLoop, calls=%fused_computation.74 | loop fusion | flops 2764800 | bytes 1576960 | tf_op jit(solution)/shard_map/convert_element_type | solution.py:69
  67.1 8.3 %all-to-all-start.1 = ((bf16[16,1,75,128]{3,2,1,0:T(8,128)(2,1)}), bf16[16,1,75,128]{3,2,1,0:T(8,128)(2,1)S(1)}, u32[]{:S(2)}, u32[]{:S(2)}) async-start(bf16[16,1,75,128]{3,2,1,0:T(8,128)(2,1)} %fusion.33), calls=%async_computation.1 | async-start | bytes 655360 | tf_op jit(solution)/shard_map/all_to_all | solution.py:128
  75.5 11.0 %all-to-all-done.1 = bf16[16,1,75,128]{3,2,1,0:T(8,128)(2,1)S(1)} async-done(((bf16[16,1,75,128]{3,2,1,0:T(8,128)(2,1)}), bf16[16,1,75,128]{3,2,1,0:T(8,128)(2,1)S(1)}, u32[]{:S(2)}, u32[]{:S(2)}) %all-to-all-start.1) | async-done | bytes 307232 | tf_op jit(solution)/shard_map/all_to_all | solution.py:128
  86.5 0.8 copy.23
  (66 shorter events, 10.1 us)
Async XLA Ops:
  0.6 34.4 %copy-start = (f32[75,75]{1,0:T(8,128)S(1)}, f32[75,75]{1,0:T(8,128)}, u32[]{:S(2)}) copy-start(f32[75,75]{1,0:T(8,128)} %param.13) | copy-start | bytes 67504
  1.4 16.4 %collective-permute-start = (f32[8,256]{1,0:T(8,128)S(1)}, f32[8,256]{1,0:T(8,128)S(1)}, u32[]{:S(2)}, u32[]{:S(2)}) collective-permute-start(f32[8,256]{1,0:T(8,128)S(1)} %convert_multiply_fusion), channel_id=1, source_target_pairs={{0,1},{1,2},{2,3},{3,4},{4,5},{5,6},{6,7},{7,8},{8,9},{9,10},{10,1... | collective-permute-start | bytes 24584 | tf_op jit(solution)/shard_map/ppermute | solution.py:14
  3.7 14.0 %collective-permute-start.1 = (f32[8,256]{1,0:T(8,128)S(1)}, f32[8,256]{1,0:T(8,128)S(1)}, u32[]{:S(2)}, u32[]{:S(2)}) collective-permute-start(f32[8,256]{1,0:T(8,128)S(1)} %convert_multiply_fusion), channel_id=1, source_target_pairs={{1,0},{2,1},{3,2},{4,3},{5,4},{6,5},{7,6},{8,7},{9,8},{10,9},{11,1... | collective-permute-start | bytes 24584 | tf_op jit(solution)/shard_map/ppermute | solution.py:17
  7.1 30.3 %all-to-all-start = ((f32[1,16,3,128]{3,2,0,1:T(4,128)}), f32[1,16,3,128]{3,2,0,1:T(4,128)S(1)}, u32[]{:S(2)}, u32[]{:S(2)}) async-start(f32[1,16,3,128]{3,2,0,1:T(4,128)} %pad_maximum_fusion.1), calls=%async_computation | async-start | bytes 65536 | tf_op jit(solution)/shard_map/all_to_all | solution.py:131
  34.8 1.2 %copy-start.2 = (f32[8,256]{1,0:T(8,128)S(1)}, f32[8,256]{1,0:T(8,128)}, u32[]{:S(2)}) copy-start(f32[8,256]{1,0:T(8,128)} %param.14) | copy-start | bytes 24580
  36.0 10.1 %copy-start.1 = (bf16[75,8,256]{2,1,0:T(8,128)(2,1)}, bf16[75,8,256]{2,1,0:T(8,128)(2,1)S(1)}, u32[]{:S(2)}) copy-start(bf16[75,8,256]{2,1,0:T(8,128)(2,1)S(1)} %fusion.30) | copy-start | bytes 921604
  36.1 3.2 %collective-permute-start.2 = (bf16[75,1,256]{2,1,0:T(2,128)(2,1)S(1)}, bf16[75,1,256]{2,1,0:T(2,128)(2,1)S(1)}, u32[]{:S(2)}, u32[]{:S(2)}) collective-permute-start(bf16[75,1,256]{2,1,0:T(2,128)(2,1)S(1)} %slice.437), channel_id=1, source_target_pairs={{1,0},{2,1},{3,2},{4,3},{5,4},{6,5},{7,6},{8,7},{9,8},{10,9},{11,1... | collective-permute-start | bytes 115208 | tf_op jit(solution)/shard_map/ppermute | solution.py:25
  65.5 9.9 %copy-start.3 = (s32[1,16]{1,0:T(1,128)S(1)}, s32[1,16]{1,0:T(1,128)}, u32[]{:S(2)}) copy-start(s32[1,16]{1,0:T(1,128)} %param.17) | copy-start | bytes 196
  67.1 19.4 %all-to-all-start.1 = ((bf16[16,1,75,128]{3,2,1,0:T(8,128)(2,1)}), bf16[16,1,75,128]{3,2,1,0:T(8,128)(2,1)S(1)}, u32[]{:S(2)}, u32[]{:S(2)}) async-start(bf16[16,1,75,128]{3,2,1,0:T(8,128)(2,1)} %fusion.33), calls=%async_computation.1 | async-start | bytes 655360 | tf_op jit(solution)/shard_map/all_to_all | solution.py:128
where the time goes:
time: 87.9 us; the launch traced here: 87.3 us
  local copies, waits for them, and re-layouts  29.1 us (33%)
  starting transfers between devices  22.5 us (26%)
  other arithmetic  21 us (24%)
  waiting for transfers between devices  12.8 us (15%)
  between operations  1.14 us (1%)
    all_to_all x1, waiting for transfers between devices, body(): lax.all_to_all(answer_probes(flat_field, lax.all_to_all(probes, 'tile', s...  11 us
    all_to_all x1, starting transfers between devices, body(): lax.all_to_all(probes, 'tile', split_axis=1, concat_axis=0, tiled=True)  9.3 us
    all_to_all x1, starting transfers between devices, body(): lax.all_to_all(answer_probes(flat_field, lax.all_to_all(probes, 'tile', s...  8.28 us
    add x8, other arithmetic, diffuse(): padded[:, 1:-1] + (flux_rows[:, 1:] - flux_rows[:, :-1]) + net_cols[:, 1:-1]  7.73 us
    gather x2, local copies, waits for them, and re-layouts, bilinear(): corner_ne = jnp.take(flat_field, anchor + 1, axis=1).astype(jnp.float32)  6.47 us
    gather x2, local copies, waits for them, and re-layouts, bilinear(): jnp.take(flat_field, anchor + columns + 1, axis=1).astype(jnp.float32)  6.47 us
    gather x2, local copies, waits for them, and re-layouts, bilinear(): jnp.take(flat_field, anchor + columns, axis=1).astype(jnp.float32)  6.47 us
    gather x2, local copies, waits for them, and re-layouts, bilinear(): corner_nw = jnp.take(flat_field, anchor, axis=1).astype(jnp.float32)  6.47 us
  transfers between devices with their start and end apart: 5, of which 2 were waited for; matrix products, arithmetic and copies ran while one was open for 25% of the time, Pallas kernels for 0%

commit v1 on v0

v1 whole, which is shorter than its diff:
```python
import functools

import jax
import jax.numpy as jnp
from jax import lax
from jax.experimental import pallas as pl
from jax.experimental.pallas import tpu as pltpu
from jax.sharding import PartitionSpec as P

STEPS = 8
GROUP = 8
SPREAD = 3.4641016151377544
MESH = pl.DeviceIdType.MESH


def scramble(hashed):
    hashed = (hashed ^ lax.shift_right_logical(hashed, jnp.int32(16))) * jnp.int32(-2048144789)
    hashed = (hashed ^ lax.shift_right_logical(hashed, jnp.int32(13))) * jnp.int32(-1028477387)
    return hashed ^ lax.shift_right_logical(hashed, jnp.int32(16))


def kernel(
    n,
    seeds_ref,
    count_ref,
    diff_ref,
    wet_ref,
    vert_ref,
    scale_ref,
    cell_ref,
    frac_ref,
    pert_ref,
    prof_ref,
    edge_send,
    above_recv,
    below_recv,
    next_recv,
    probe_send,
    probe_recv,
    noise,
    face_rows,
    face_cols,
    wet_all,
    state,
    vert_pad,
    field,
    field_rows,
    prof_send,
    prof_recv,
    edge_ss,
    edge_rs,
    probe_ss,
    probe_rs,
    prof_ss,
    prof_rs,
):
    me = lax.axis_index("tile")
    rows, cols = diff_ref.shape
    levels = vert_ref.shape[0]
    padded = state.shape[1]
    groups = padded // GROUP
    slots = cell_ref.shape[2]
    total_rows = n * rows
    span = rows + 2 * STEPS + 1
    kept = rows + 1

    barrier = pltpu.get_barrier_semaphore()

    def greet(k, carry):
        peer = lax.rem(me + k, n)
        pl.semaphore_signal(barrier, inc=1, device_id={"tile": peer}, device_id_type=MESH)
        return carry

    lax.fori_loop(1, n, greet, 0)

    kappa = diff_ref[...] * wet_ref[...].astype(jnp.float32)
    edge_send[0:rows, :] = kappa
    edge_send[rows : 2 * rows, :] = scale_ref[...]
    slot_ids = lax.broadcasted_iota(jnp.int32, (1, slots), 1)

    def pack(h, carry):
        anchor = cell_ref[0, pl.ds(h, 1), :]
        frac = frac_ref[0, h]
        row = lax.shift_right_logical(anchor, jnp.int32(cols.bit_length() - 1))
        col = anchor - row * cols
        live = jnp.where(slot_ids < count_ref[0, h], 1.0, 0.0)
        frac_y = frac[0:1, :]
        probe_send[h, 0:1, :] = col.astype(jnp.float32)
        probe_send[h, 1:2, :] = frac[1:2, :]
        probe_send[h, 2:3, :] = row.astype(jnp.float32)
        probe_send[h, 3:4, :] = (1.0 - frac_y) * live
        probe_send[h, 4:5, :] = frac_y * live
        probe_send[h, 5:8, :] = jnp.zeros((3, slots), jnp.float32)
        return carry

    lax.fori_loop(0, n, pack, 0)

    seed_a = seeds_ref[0]
    seed_b = seeds_ref[1]
    shape = (GROUP, cols)
    spread_ids = (
        lax.broadcasted_iota(jnp.int32, shape, 0) * (total_rows * cols)
        + lax.broadcasted_iota(jnp.int32, shape, 1)
    ) * jnp.int32(-1640531535)
    first_row = me * rows - STEPS

    def draw(g, carry):
        at = pl.multiple_of(g * GROUP, GROUP)
        for j in range(span):
            base = (g * (GROUP * total_rows) + first_row + j) * cols
            hashed = scramble(spread_ids + (base * jnp.int32(-1640531535) + seed_a))
            hashed = scramble(hashed ^ seed_b)
            drawn = lax.shift_right_logical(hashed, jnp.int32(8)).astype(jnp.float32)
            noise[j, pl.ds(at, GROUP), :] = drawn * (SPREAD / 16777216.0) + SPREAD * (
                0.5 / 16777216.0 - 0.5
            )
        return carry

    lax.fori_loop(0, groups // 2, draw, 0)

    pl.semaphore_wait(barrier, n - 1)

    def edge_copy(which):
        if which == 0:
            src, dst, by = edge_send.at[pl.ds(0, rows)], above_recv, 1
        elif which == 1:
            src, dst, by = edge_send, below_recv, n - 1
        else:
            src, dst, by = edge_send.at[pl.ds(0, rows)], next_recv, n - 2
        return pltpu.make_async_remote_copy(
            src_ref=src,
            dst_ref=dst,
            send_sem=edge_ss.at[which],
            recv_sem=edge_rs.at[which],
            device_id={"tile": lax.rem(me + by, n)},
            device_id_type=MESH,
        )

    def probe_copy(peer, slot):
        return pltpu.make_async_remote_copy(
            src_ref=probe_send.at[peer],
            dst_ref=probe_recv.at[slot],
            send_sem=probe_ss.at[peer],
            recv_sem=probe_rs.at[slot],
            device_id={"tile": peer},
            device_id_type=MESH,
        )

    for which in range(3):
        edge_copy(which).start()

    def send_probe(k, carry):
        probe_copy(lax.rem(me + k, n), me).start()
        return carry

    lax.fori_loop(1, n, send_probe, 0)
    probe_recv[me] = probe_send[me]

    lax.fori_loop(groups // 2, groups, draw, 0)

    vert_pad[...] = jnp.zeros_like(vert_pad)
    vert_pad[0:levels, 0:levels] = vert_ref[...]
    vert = vert_pad[:, 0:padded]
    vert_hi = vert.astype(jnp.bfloat16)
    vert_lo = (vert - vert_hi.astype(jnp.float32)).astype(jnp.bfloat16)

    for which in range(3):
        edge_copy(which).wait_recv()

    zero = jnp.zeros((rows, cols), jnp.float32)
    kappa_all = jnp.concatenate(
        [
            jnp.where(me > 0, above_recv[...], zero),
            edge_send[0:rows, :],
            jnp.where(me < n - 1, below_recv[0:rows, :], zero),
            jnp.where(me < n - 2, next_recv[...], zero),
        ],
        0,
    )
    wet = jnp.where(kappa_all > 0.0, 1.0, 0.0)
    kappa_next = pltpu.roll(kappa_all, cols - 1, 1)
    last = lax.broadcasted_iota(jnp.int32, kappa_all.shape, 1) == cols - 1
    faces_c = jnp.where(last, 0.0, jnp.sqrt(kappa_all * kappa_next))
    faces_r = jnp.sqrt(kappa_all[0 : span - 1] * kappa_all[1:span])
    for j in range(span):
        wet_all[j] = jnp.broadcast_to(wet[j : j + 1], shape)
        face_cols[j] = jnp.broadcast_to(faces_c[j : j + 1], shape)
        if j < span - 1:
            face_rows[j] = jnp.broadcast_to(faces_r[j : j + 1], shape)

    def diffuse(g, carry):
        at = pl.multiple_of(g * GROUP, GROUP)
        old = [noise[j, pl.ds(at, GROUP), :] * wet_all[j] for j in range(span)]
        for step in range(STEPS):
            new = list(old)
            flux_up = face_rows[step] * (old[step + 1] - old[step])
            for j in range(step + 1, span - 1 - step):
                here = old[j]
                flux_down = face_rows[j] * (old[j + 1] - here)
                flux = face_cols[j] * (pltpu.roll(here, cols - 1, 1) - here)
                new[j] = here + (flux_down - flux_up) + (flux - pltpu.roll(flux, 1, 1))
                flux_up = flux_down
            old = new
        for r in range(kept):
            state[r, pl.ds(at, GROUP), :] = old[STEPS + r]
        return carry

    lax.fori_loop(0, groups, diffuse, 0)

    for r in range(kept):
        value = state[r]
        high = value.astype(jnp.bfloat16)
        low = (value - high.astype(jnp.float32)).astype(jnp.bfloat16)
        dot = functools.partial(jnp.dot, preferred_element_type=jnp.float32)
        mixed = dot(vert_hi, high) + (dot(vert_hi, low) + dot(vert_lo, high))
        if r < rows:
            scale = scale_ref[r : r + 1, :]
        else:
            scale = below_recv[rows : rows + 1, :]
        field[r * padded : (r + 1) * padded, :] = (mixed * scale).astype(jnp.bfloat16)

    def await_probe(k, carry):
        source = lax.rem(me + k, n)
        probe_copy(source, source).wait_recv()
        return carry

    lax.fori_loop(1, n, await_probe, 0)

    col_ids = lax.broadcasted_iota(jnp.int32, (cols, 2 * slots), 0).astype(jnp.float32)

    def answer(pair):
        probes = jnp.concatenate([probe_recv[2 * pair], probe_recv[2 * pair + 1]], 1)
        col, frac_x, row = probes[0:1], probes[1:2], probes[2:3]
        top, bottom = probes[3:4], probes[4:5]
        weights = jnp.where(
            col_ids == col, 1.0 - frac_x, jnp.where(col_ids == col + 1.0, frac_x, 0.0)
        ).astype(jnp.bfloat16)
        across = jnp.dot(field[...], weights, preferred_element_type=jnp.float32)
        total = None
        for r in range(kept):
            share = jnp.where(row == float(r), top, jnp.where(row == float(r - 1), bottom, 0.0))
            term = across[r * padded : (r + 1) * padded] * share
            total = term if total is None else total + term
        total = total.astype(jnp.bfloat16)
        prof_send[2 * pair] = total[:, 0:slots]
        prof_send[2 * pair + 1] = total[:, slots : 2 * slots]

    def prof_copy(peer, slot):
        return pltpu.make_async_remote_copy(
            src_ref=prof_send.at[peer],
            dst_ref=prof_recv.at[slot],
            send_sem=prof_ss.at[peer],
            recv_sem=prof_rs.at[slot],
            device_id={"tile": peer},
            device_id_type=MESH,
        )

    pairs = n // 2
    my_pair = me // 2

    def answer_other(k, carry):
        pair = lax.rem(my_pair + k, pairs)
        answer(pair)
        prof_copy(2 * pair, me).start()
        prof_copy(2 * pair + 1, me).start()
        return carry

    lax.fori_loop(1, pairs, answer_other, 0)
    answer(my_pair)
    prof_copy(4 * my_pair + 1 - me, me).start()
    prof_ref[0, me] = prof_send[me, 0:levels, :]

    for r in range(rows):
        field_rows[:, r, :] = field[r * padded : (r + 1) * padded, :].astype(jnp.float32)
    pert_ref[...] = field_rows[0:levels].astype(jnp.bfloat16)

    def finish(k, carry):
        source = lax.rem(me + n - k, n)
        prof_copy(source, source).wait_recv()
        prof_ref[0, source] = prof_recv[source, 0:levels, :]
        return carry

    lax.fori_loop(1, n, finish, 0)

    def settle(k, carry):
        peer = lax.rem(me + k, n)
        probe_copy(peer, me).wait_send()
        prof_copy(peer, me).wait_send()
        return carry

    lax.fori_loop(1, n, settle, 0)
    for which in range(3):
        edge_copy(which).wait_send()


def body(
    noise_seeds, diffusivity, wet_mask, vert_factor, norm_scale, obs_cell, obs_frac, obs_count
):
    rows, cols = diffusivity.shape
    levels = vert_factor.shape[0]
    n = lax.axis_size("tile")
    slots = obs_cell.shape[2]
    if rows != STEPS or n % 2 or cols & (cols - 1):
        raise ValueError("unsupported sizes")
    padded = -(-levels // 16) * 16
    span = rows + 2 * STEPS + 1
    kept = rows + 1
    f32, bf16 = jnp.float32, jnp.bfloat16
    vmem = pl.BlockSpec(memory_space=pltpu.VMEM)
    smem = pl.BlockSpec(memory_space=pltpu.SMEM)
    dma = pltpu.SemaphoreType.DMA
    return pl.pallas_call(
        functools.partial(kernel, n),
        out_shape=(
            jax.ShapeDtypeStruct((levels, rows, cols), bf16),
            jax.ShapeDtypeStruct((1, n, levels, slots), bf16),
        ),
        in_specs=[smem, smem] + [vmem] * 6,
        out_specs=(vmem, vmem),
        scratch_shapes=[
            pltpu.VMEM((2 * rows, cols), f32),
            pltpu.VMEM((rows, cols), f32),
            pltpu.VMEM((2 * rows, cols), f32),
            pltpu.VMEM((rows, cols), f32),
            pltpu.VMEM((n, 8, slots), f32),
            pltpu.VMEM((n, 8, slots), f32),
            pltpu.VMEM((span, padded, cols), f32),
            pltpu.VMEM((span, GROUP, cols), f32),
            pltpu.VMEM((span, GROUP, cols), f32),
            pltpu.VMEM((span, GROUP, cols), f32),
            pltpu.VMEM((kept, padded, cols), f32),
            pltpu.VMEM((padded, 128), f32),
            pltpu.VMEM((kept * padded, cols), bf16),
            pltpu.VMEM((padded, rows, cols), f32),
            pltpu.VMEM((n, padded, slots), bf16),
            pltpu.VMEM((n, padded, slots), bf16),
            dma((3,)),
            dma((3,)),
            dma((n,)),
            dma((n,)),
            dma((n,)),
            dma((n,)),
        ],
        compiler_params=pltpu.CompilerParams(
            collective_id=0, has_side_effects=True, vmem_limit_bytes=32 * 1024 * 1024
        ),
    )(
        noise_seeds,
        obs_count,
        diffusivity,
        wet_mask,
        vert_factor,
        norm_scale,
        obs_cell,
        obs_frac,
    )


def solution(mesh):
    in_specs = (
        P("member"),
        P("tile", None),
        P("tile", None),
        P(),
        P("tile", None),
        P("tile", None, None),
        P("tile", None, None, None),
        P("tile", None),
    )
    out_specs = (P("member", "tile", None), P("tile", None, "member", None))
    return jax.shard_map(body, mesh=mesh, in_specs=in_specs, out_specs=out_specs, check_vma=False)
```

time: 87.9 us -> 41.4 us (0.47)
  the two profiles are of different devices: /device:TPU:0 before, /device:TPU:9 now
where the time goes in v1:
time: 41.4 us; the launch traced here: 40.9 us
  Pallas kernels  33.2 us (80%)
  local copies, waits for them, and re-layouts  7.1 us (17%)
  between operations  0.66 us (2%)
    pallas_call x1, Pallas kernels, body(): pl.pallas_call(functools.partial(kernel, n), out_shape=(jax.ShapeDtypeStr...  33.2 us
    unnamed x17, local copies, waits for them, and re-layouts  6.3 us

profile of v1, /device:TPU:9, one launch (start us, length us, event | category | flops | bytes accessed | tf_op | source)
XLA Modules:
  0.0 40.9 jit_solution(14558089671635202901)
XLA Ops:
  0.6 0.0 copy-start
  0.6 0.8 %copy-done = f32[75,75]{1,0:T(8,128)S(1)} copy-done((f32[75,75]{1,0:T(8,128)S(1)}, f32[75,75]{1,0:T(8,128)}, u32[]{:S(2)}) %copy-start) | copy-done | bytes 22524
  1.4 0.0 copy-start.1
  1.4 0.7 %copy-done.1 = f32[1,16,2,128]{3,2,1,0:T(2,128)S(1)} copy-done((f32[1,16,2,128]{3,2,1,0:T(2,128)S(1)}, f32[1,16,2,128]{3,2,1,0:T(2,128)}, u32[]{:S(2)}) %copy-start.1) | copy-done | bytes 16408
  2.1 0.0 copy-start.2
  2.1 0.7 %copy-done.2 = f32[8,256]{1,0:T(8,128)S(1)} copy-done((f32[8,256]{1,0:T(8,128)S(1)}, f32[8,256]{1,0:T(8,128)}, u32[]{:S(2)}) %copy-start.2) | copy-done | bytes 8216
  2.8 0.0 copy-start.3
  2.8 0.7 %copy-done.3 = s32[8,256]{1,0:T(8,128)S(1)} copy-done((s32[8,256]{1,0:T(8,128)S(1)}, s32[8,256]{1,0:T(8,128)}, u32[]{:S(2)}) %copy-start.3) | copy-done | bytes 8216
  3.5 0.0 copy-start.4
  3.5 0.7 %copy-done.4 = f32[8,256]{1,0:T(8,128)S(1)} copy-done((f32[8,256]{1,0:T(8,128)S(1)}, f32[8,256]{1,0:T(8,128)}, u32[]{:S(2)}) %copy-start.4) | copy-done | bytes 8216
  4.2 0.0 copy-start.5
  4.2 0.7 %copy-done.5 = s32[1,16,128]{2,1,0:T(8,128)S(1)} copy-done((s32[1,16,128]{2,1,0:T(8,128)S(1)}, s32[1,16,128]{2,1,0:T(8,128)}, u32[]{:S(2)}) %copy-start.5) | copy-done | bytes 8216
  4.9 0.0 copy-start.6
  4.9 0.7 %copy-done.6 = s32[2]{0:T(128)S(1)} copy-done((s32[2]{0:T(128)S(1)}, s32[2]{0:T(128)}, u32[]{:S(2)}) %copy-start.6) | copy-done | bytes 32
  5.6 0.0 copy-start.7
  5.6 0.7 %copy-done.7 = s32[1,16]{1,0:T(1,128)S(1)} copy-done((s32[1,16]{1,0:T(1,128)S(1)}, s32[1,16]{1,0:T(1,128)}, u32[]{:S(2)}) %copy-start.7) | copy-done | bytes 88
  6.2 33.2 %shard_map.95 = (bf16[75,8,256]{2,1,0:T(8,128)(2,1)S(1)}, bf16[1,16,75,128]{3,2,1,0:T(8,128)(2,1)S(1)}) custom-call(s32[2]{0:T(128)S(1)} %copy-done.6, s32[1,16]{1,0:T(1,128)S(1)} %copy-done.7, f32[8,256]{1,0:T(8,128)S(1)} %copy-done.2, s32[8,256]{1,0:T(8,128)S(1)} %copy-done.3, f32[75,75]{1,0:T(8,128)S(1)} %copy-done, f32[8,256]{1,0:T(8,128)S(1)} %copy-done.4, ...), custom_call_target="tpu_custom_call" | custom-call | tf_op jit(solution)/shard_map/pallas_call | solution.py:312
  39.4 0.8 %copy.10 = bf16[1,16,75,128]{3,1,2,0:T(8,128)(2,1)} copy(bf16[1,16,75,128]{3,2,1,0:T(8,128)(2,1)S(1)} %get-tuple-element.3) | data formatting | bytes 614400 | tf_op jit(solution)/shard_map/pallas_call | solution.py:312
  40.2 0.7 %copy.12 = bf16[75,8,256]{2,1,0:T(8,128)(2,1)} copy(bf16[75,8,256]{2,1,0:T(8,128)(2,1)S(1)} %get-tuple-element.6) | data formatting | bytes 614400
Async XLA Ops:
  0.6 0.8 %copy-start = (f32[75,75]{1,0:T(8,128)S(1)}, f32[75,75]{1,0:T(8,128)}, u32[]{:S(2)}) copy-start(f32[75,75]{1,0:T(8,128)} %vert_ref.1) | copy-start | bytes 67504
  1.4 0.7 %copy-start.1 = (f32[1,16,2,128]{3,2,1,0:T(2,128)S(1)}, f32[1,16,2,128]{3,2,1,0:T(2,128)}, u32[]{:S(2)}) copy-start(f32[1,16,2,128]{3,2,1,0:T(2,128)} %frac_ref.1) | copy-start | bytes 49156
  2.1 0.7 %copy-start.2 = (f32[8,256]{1,0:T(8,128)S(1)}, f32[8,256]{1,0:T(8,128)}, u32[]{:S(2)}) copy-start(f32[8,256]{1,0:T(8,128)} %diff_ref.1) | copy-start | bytes 24580
  2.8 0.7 %copy-start.3 = (s32[8,256]{1,0:T(8,128)S(1)}, s32[8,256]{1,0:T(8,128)}, u32[]{:S(2)}) copy-start(s32[8,256]{1,0:T(8,128)} %wet_ref.1) | copy-start | bytes 24580
  3.5 0.7 %copy-start.4 = (f32[8,256]{1,0:T(8,128)S(1)}, f32[8,256]{1,0:T(8,128)}, u32[]{:S(2)}) copy-start(f32[8,256]{1,0:T(8,128)} %scale_ref.1) | copy-start | bytes 24580
  4.2 0.7 %copy-start.5 = (s32[1,16,128]{2,1,0:T(8,128)S(1)}, s32[1,16,128]{2,1,0:T(8,128)}, u32[]{:S(2)}) copy-start(s32[1,16,128]{2,1,0:T(8,128)} %cell_ref.1) | copy-start | bytes 24580
  4.9 0.7 %copy-start.6 = (s32[2]{0:T(128)S(1)}, s32[2]{0:T(128)}, u32[]{:S(2)}) copy-start(s32[2]{0:T(128)} %seeds_ref.1) | copy-start | bytes 28
  5.6 0.7 %copy-start.7 = (s32[1,16]{1,0:T(1,128)S(1)}, s32[1,16]{1,0:T(1,128)}, u32[]{:S(2)}) copy-start(s32[1,16]{1,0:T(1,128)} %count_ref.1) | copy-start | bytes 196

commit v2 on v1

--- a/solution.py
+++ b/solution.py
@@ -21,6 +21,16 @@
 
 def kernel(
     n,
+    seeds_hbm,
+    count_hbm,
+    diff_hbm,
+    wet_hbm,
+    vert_hbm,
+    scale_hbm,
+    cell_hbm,
+    frac_hbm,
+    pert_ref,
+    prof_ref,
     seeds_ref,
     count_ref,
     diff_ref,
@@ -29,8 +39,7 @@
     scale_ref,
     cell_ref,
     frac_ref,
-    pert_ref,
-    prof_ref,
+    in_sems,
     edge_send,
     above_recv,
     below_recv,
@@ -54,6 +63,24 @@
     prof_ss,
     prof_rs,
 ):
+    pulls = [
+        pltpu.make_async_copy(src, dst, in_sems.at[k])
+        for k, (src, dst) in enumerate(
+            (
+                (diff_hbm, diff_ref),
+                (wet_hbm, wet_ref),
+                (scale_hbm, scale_ref),
+                (seeds_hbm, seeds_ref),
+                (count_hbm, count_ref),
+                (cell_hbm, cell_ref),
+                (frac_hbm, frac_ref),
+                (vert_hbm, vert_ref),
+            )
+        )
+    ]
+    for pull in pulls:
+        pull.start()
+
     me = lax.axis_index("tile")
     rows, cols = diff_ref.shape
     levels = vert_ref.shape[0]
@@ -72,6 +99,9 @@
         return carry
 
     lax.fori_loop(1, n, greet, 0)
+
+    for pull in pulls:
+        pull.wait()
 
     kappa = diff_ref[...] * wet_ref[...].astype(jnp.float32)
     edge_send[0:rows, :] = kappa
@@ -307,7 +337,7 @@
     kept = rows + 1
     f32, bf16 = jnp.float32, jnp.bfloat16
     vmem = pl.BlockSpec(memory_space=pltpu.VMEM)
-    smem = pl.BlockSpec(memory_space=pltpu.SMEM)
+    hbm = pl.BlockSpec(memory_space=pltpu.HBM)
     dma = pltpu.SemaphoreType.DMA
     return pl.pallas_call(
         functools.partial(kernel, n),
@@ -315,9 +345,18 @@
             jax.ShapeDtypeStruct((levels, rows, cols), bf16),
             jax.ShapeDtypeStruct((1, n, levels, slots), bf16),
         ),
-        in_specs=[smem, smem] + [vmem] * 6,
+        in_specs=[hbm] * 8,
         out_specs=(vmem, vmem),
         scratch_shapes=[
+            pltpu.SMEM(noise_seeds.shape, jnp.int32),
+            pltpu.SMEM(obs_count.shape, jnp.int32),
+            pltpu.VMEM(diffusivity.shape, f32),
+            pltpu.VMEM(wet_mask.shape, jnp.int32),
+            pltpu.VMEM(vert_factor.shape, f32),
+            pltpu.VMEM(norm_scale.shape, f32),
+            pltpu.VMEM(obs_cell.shape, jnp.int32),
+            pltpu.VMEM(obs_frac.shape, f32),
+            dma((8,)),
             pltpu.VMEM((2 * rows, cols), f32),
             pltpu.VMEM((rows, cols), f32),
             pltpu.VMEM((2 * rows, cols), f32),
@@ -342,7 +381,7 @@
             dma((n,)),
         ],
         compiler_params=pltpu.CompilerParams(
-            collective_id=0, has_side_effects=True, vmem_limit_bytes=32 * 1024 * 1024
+            collective_id=0, has_side_effects=True, vmem_limit_bytes=60 * 1024 * 1024
         ),
     )(
         noise_seeds,

time: 41.4 us -> 36.8 us (0.89)
  the two profiles are of different devices: /device:TPU:9 before, /device:TPU:0 now
where the time goes in v2:
time: 36.8 us; the launch traced here: 36.3 us
  Pallas kernels  33.1 us (90%)
  local copies, waits for them, and re-layouts  2.54 us (7%)
  between operations  0.65 us (2%)
    pallas_call x1, Pallas kernels, body(): pl.pallas_call(functools.partial(kernel, n), out_shape=(jax.ShapeDtypeStr...  33.1 us
    pallas_call x1, local copies, waits for them, and re-layouts, body(): pl.pallas_call(functools.partial(kernel, n), out_shape=(jax.ShapeDtypeStr...  1.81 us

profile of v2, /device:TPU:0, one launch (start us, length us, event | category | flops | bytes accessed | tf_op | source)
XLA Modules:
  0.0 36.3 jit_solution(1541343407432737945)
XLA Ops:
  0.6 33.1 %shard_map.95 = (bf16[75,8,256]{2,1,0:T(8,128)(2,1)}, bf16[1,16,75,128]{3,2,1,0:T(8,128)(2,1)}) custom-call(s32[2]{0:T(128)} %seeds_hbm.1, s32[1,16]{1,0:T(1,128)} %count_hbm.1, f32[8,256]{1,0:T(8,128)} %diff_hbm.1, s32[8,256]{1,0:T(8,128)} %wet_hbm.1, f32[75,75]{1,0:T(8,128)} %vert_hbm.1, f32[8,256]{1,0:T(8,128)} %scale_hbm.1, s32[1,16,128]{2,1,0:T(8,128)} %cell_hbm.1, ...), custom_call_target="tpu_custom_call" | custom-call | tf_op jit(solution)/shard_map/pallas_call | solution.py:342
  33.8 0.0 copy-start
  33.8 1.8 %copy.10 = bf16[1,16,75,128]{3,1,2,0:T(8,128)(2,1)} copy(bf16[1,16,75,128]{3,2,1,0:T(8,128)(2,1)} %get-tuple-element.3) | data formatting | bytes 614400 | tf_op jit(solution)/shard_map/pallas_call | solution.py:342
  35.6 0.0 copy-done
  35.6 0.7 %copy.12 = bf16[75,8,256]{2,1,0:T(8,128)(2,1)} copy(bf16[75,8,256]{2,1,0:T(8,128)(2,1)S(1)} %copy-done) | data formatting | bytes 614400
Async XLA Ops:
  33.8 1.8 %copy-start = (bf16[75,8,256]{2,1,0:T(8,128)(2,1)S(1)}, bf16[75,8,256]{2,1,0:T(8,128)(2,1)}, u32[]{:S(2)}) copy-start(bf16[75,8,256]{2,1,0:T(8,128)(2,1)} %get-tuple-element.6) | copy-start | bytes 921604

commit v3 on v2

--- a/solution.py
+++ b/solution.py
@@ -50,10 +50,15 @@
     face_rows,
     face_cols,
     wet_all,
+    scale_all,
     state,
     vert_pad,
+    scaled,
+    weights,
+    shares,
     field,
     field_rows,
+    prof_rows,
     prof_send,
     prof_recv,
     edge_ss,
@@ -83,6 +88,7 @@
 
     me = lax.axis_index("tile")
     rows, cols = diff_ref.shape
+    half = cols // 2
     levels = vert_ref.shape[0]
     padded = state.shape[1]
     groups = padded // GROUP
@@ -104,8 +110,16 @@
         pull.wait()
 
     kappa = diff_ref[...] * wet_ref[...].astype(jnp.float32)
-    edge_send[0:rows, :] = kappa
-    edge_send[rows : 2 * rows, :] = scale_ref[...]
+    pair_shape = (cols, cols)
+    lane = lax.broadcasted_iota(jnp.int32, pair_shape, 1)
+    lane = jnp.where(lane < half, 2 * lane, 2 * lane - (cols - 1))
+    split = jnp.where(lax.broadcasted_iota(jnp.int32, pair_shape, 0) == lane, 1.0, 0.0)
+    edge_send[...] = jnp.dot(
+        jnp.concatenate([kappa, scale_ref[...]], 0),
+        split,
+        precision=lax.Precision.HIGHEST,
+        preferred_element_type=jnp.float32,
+    )
     slot_ids = lax.broadcasted_iota(jnp.int32, (1, slots), 1)
 
     def pack(h, carry):
@@ -113,14 +127,11 @@
         frac = frac_ref[0, h]
         row = lax.shift_right_logical(anchor, jnp.int32(cols.bit_length() - 1))
         col = anchor - row * cols
-        live = jnp.where(slot_ids < count_ref[0, h], 1.0, 0.0)
-        frac_y = frac[0:1, :]
         probe_send[h, 0:1, :] = col.astype(jnp.float32)
         probe_send[h, 1:2, :] = frac[1:2, :]
         probe_send[h, 2:3, :] = row.astype(jnp.float32)
-        probe_send[h, 3:4, :] = (1.0 - frac_y) * live
-        probe_send[h, 4:5, :] = frac_y * live
-        probe_send[h, 5:8, :] = jnp.zeros((3, slots), jnp.float32)
+        probe_send[h, 3:4, :] = frac[0:1, :]
+        probe_send[h, 4:8, :] = jnp.zeros((4, slots), jnp.float32)
         return carry
 
     lax.fori_loop(0, n, pack, 0)
@@ -128,9 +139,10 @@
     seed_a = seeds_ref[0]
     seed_b = seeds_ref[1]
     shape = (GROUP, cols)
+    col_ids = lax.broadcasted_iota(jnp.int32, shape, 1)
+    col_ids = jnp.where(col_ids < half, 2 * col_ids, 2 * col_ids - (cols - 1))
     spread_ids = (
-        lax.broadcasted_iota(jnp.int32, shape, 0) * (total_rows * cols)
-        + lax.broadcasted_iota(jnp.int32, shape, 1)
+        lax.broadcasted_iota(jnp.int32, shape, 0) * (total_rows * cols) + col_ids
     ) * jnp.int32(-1640531535)
     first_row = me * rows - STEPS
 
@@ -208,46 +220,20 @@
         0,
     )
     wet = jnp.where(kappa_all > 0.0, 1.0, 0.0)
-    kappa_next = pltpu.roll(kappa_all, cols - 1, 1)
-    last = lax.broadcasted_iota(jnp.int32, kappa_all.shape, 1) == cols - 1
-    faces_c = jnp.where(last, 0.0, jnp.sqrt(kappa_all * kappa_next))
+    even, odd = kappa_all[:, 0:half], kappa_all[:, half:cols]
+    last = lax.broadcasted_iota(jnp.int32, even.shape, 1) == half - 1
+    faces_in = jnp.sqrt(even * odd)
+    faces_out = jnp.where(last, 0.0, jnp.sqrt(odd * pltpu.roll(even, half - 1, 1)))
+    faces_c = jnp.concatenate([faces_in, faces_out], 1)
     faces_r = jnp.sqrt(kappa_all[0 : span - 1] * kappa_all[1:span])
     for j in range(span):
         wet_all[j] = jnp.broadcast_to(wet[j : j + 1], shape)
         face_cols[j] = jnp.broadcast_to(faces_c[j : j + 1], shape)
         if j < span - 1:
             face_rows[j] = jnp.broadcast_to(faces_r[j : j + 1], shape)
-
-    def diffuse(g, carry):
-        at = pl.multiple_of(g * GROUP, GROUP)
-        old = [noise[j, pl.ds(at, GROUP), :] * wet_all[j] for j in range(span)]
-        for step in range(STEPS):
-            new = list(old)
-            flux_up = face_rows[step] * (old[step + 1] - old[step])
-            for j in range(step + 1, span - 1 - step):
-                here = old[j]
-                flux_down = face_rows[j] * (old[j + 1] - here)
-                flux = face_cols[j] * (pltpu.roll(here, cols - 1, 1) - here)
-                new[j] = here + (flux_down - flux_up) + (flux - pltpu.roll(flux, 1, 1))
-                flux_up = flux_down
-            old = new
-        for r in range(kept):
-            state[r, pl.ds(at, GROUP), :] = old[STEPS + r]
-        return carry
-
-    lax.fori_loop(0, groups, diffuse, 0)
-
     for r in range(kept):
-        value = state[r]
-        high = value.astype(jnp.bfloat16)
-        low = (value - high.astype(jnp.float32)).astype(jnp.bfloat16)
-        dot = functools.partial(jnp.dot, preferred_element_type=jnp.float32)
-        mixed = dot(vert_hi, high) + (dot(vert_hi, low) + dot(vert_lo, high))
-        if r < rows:
-            scale = scale_ref[r : r + 1, :]
-        else:
-            scale = below_recv[rows : rows + 1, :]
-        field[r * padded : (r + 1) * padded, :] = (mixed * scale).astype(jnp.bfloat16)
+        row = edge_send[rows + r : rows + r + 1] if r < rows else below_recv[rows : rows + 1]
+        scale_all[r] = jnp.broadcast_to(row, shape)
 
     def await_probe(k, carry):
         source = lax.rem(me + k, n)
@@ -256,66 +242,139 @@
 
     lax.fori_loop(1, n, await_probe, 0)
 
-    col_ids = lax.broadcasted_iota(jnp.int32, (cols, 2 * slots), 0).astype(jnp.float32)
-
-    def answer(pair):
+    pairs = n // 2
+    cell_ids = lax.broadcasted_iota(jnp.int32, (cols, 2 * slots), 0)
+    cell_ids = jnp.where(cell_ids < half, 2 * cell_ids, 2 * cell_ids - (cols - 1))
+    cell_ids = cell_ids.astype(jnp.float32)
+
+    def weigh(pair, carry):
         probes = jnp.concatenate([probe_recv[2 * pair], probe_recv[2 * pair + 1]], 1)
-        col, frac_x, row = probes[0:1], probes[1:2], probes[2:3]
-        top, bottom = probes[3:4], probes[4:5]
-        weights = jnp.where(
-            col_ids == col, 1.0 - frac_x, jnp.where(col_ids == col + 1.0, frac_x, 0.0)
+        col, frac_x, row, frac_y = probes[0:1], probes[1:2], probes[2:3], probes[3:4]
+        weights[pair] = jnp.where(
+            cell_ids == col, 1.0 - frac_x, jnp.where(cell_ids == col + 1.0, frac_x, 0.0)
         ).astype(jnp.bfloat16)
-        across = jnp.dot(field[...], weights, preferred_element_type=jnp.float32)
-        total = None
         for r in range(kept):
-            share = jnp.where(row == float(r), top, jnp.where(row == float(r - 1), bottom, 0.0))
-            term = across[r * padded : (r + 1) * padded] * share
-            total = term if total is None else total + term
-        total = total.astype(jnp.bfloat16)
-        prof_send[2 * pair] = total[:, 0:slots]
-        prof_send[2 * pair + 1] = total[:, slots : 2 * slots]
-
-    def prof_copy(peer, slot):
+            shares[pair, r : r + 1, :] = jnp.where(
+                row == float(r), 1.0 - frac_y, jnp.where(row == float(r - 1), frac_y, 0.0)
+            )
+        return carry
+
+    lax.fori_loop(0, pairs, weigh, 0)
+
+    def advance(at):
+        def take(ref, j, lo):
+            return ref[j, :, lo : lo + half]
+
+        old_e, old_o = [], []
+        for j in range(span):
+            old_e.append(noise[j, pl.ds(at, GROUP), 0:half] * take(wet_all, j, 0))
+            old_o.append(noise[j, pl.ds(at, GROUP), half:cols] * take(wet_all, j, half))
+        for step in range(STEPS):
+            new_e, new_o = list(old_e), list(old_o)
+            up_e = take(face_rows, step, 0) * (old_e[step + 1] - old_e[step])
+            up_o = take(face_rows, step, half) * (old_o[step + 1] - old_o[step])
+            for j in range(step + 1, span - 1 - step):
+                here_e, here_o = old_e[j], old_o[j]
+                down_e = take(face_rows, j, 0) * (old_e[j + 1] - here_e)
+                down_o = take(face_rows, j, half) * (old_o[j + 1] - here_o)
+                inner = take(face_cols, j, 0) * (here_o - here_e)
+                outer = take(face_cols, j, half) * (pltpu.roll(here_e, half - 1, 1) - here_o)
+                new_e[j] = here_e + ((down_e - up_e) + (inner - pltpu.roll(outer, 1, 1)))
+                new_o[j] = here_o + ((down_o - up_o) + (outer - inner))
+                up_e, up_o = down_e, down_o
+            old_e, old_o = new_e, new_o
+        return old_e[STEPS : STEPS + kept], old_o[STEPS : STEPS + kept]
+
+    def prof_copy(peer, slot, at, size):
         return pltpu.make_async_remote_copy(
-            src_ref=prof_send.at[peer],
-            dst_ref=prof_recv.at[slot],
+            src_ref=prof_send.at[peer, pl.ds(at, size)],
+            dst_ref=prof_recv.at[slot, pl.ds(at, size)],
             send_sem=prof_ss.at[peer],
             recv_sem=prof_rs.at[slot],
             device_id={"tile": peer},
             device_id_type=MESH,
         )
 
-    pairs = n // 2
+    block = 2 * GROUP
     my_pair = me // 2
 
-    def answer_other(k, carry):
-        pair = lax.rem(my_pair + k, pairs)
-        answer(pair)
-        prof_copy(2 * pair, me).start()
-        prof_copy(2 * pair + 1, me).start()
-        return carry
-
-    lax.fori_loop(1, pairs, answer_other, 0)
-    answer(my_pair)
-    prof_copy(4 * my_pair + 1 - me, me).start()
-    prof_ref[0, me] = prof_send[me, 0:levels, :]
-
+    def turn(b, carry):
+        first = pl.multiple_of(b * block, block)
+        for part in range(2):
+            at = pl.multiple_of(first + part * GROUP, GROUP)
+            evens, odds = advance(at)
+            for r in range(kept):
+                if r < rows:
+                    state[r, pl.ds(at, GROUP), 0:half] = evens[r]
+                    state[r, pl.ds(at, GROUP), half:cols] = odds[r]
+                line = r * block + part * GROUP
+                scaled[line : line + GROUP, 0:half] = evens[r] * scale_all[r, :, 0:half]
+                scaled[line : line + GROUP, half:cols] = odds[r] * scale_all[r, :, half:cols]
+        left = scaled[...].astype(jnp.bfloat16)
+
+        def answer(pair):
+            across = jnp.dot(left, weights[pair], preferred_element_type=jnp.float32)
+            total = None
+            for r in range(kept):
+                term = across[r * block : (r + 1) * block] * shares[pair, r : r + 1, :]
+                total = term if total is None else total + term
+            total = total.astype(jnp.bfloat16)
+            prof_send[2 * pair, pl.ds(first, block), :] = total[:, 0:slots]
+            prof_send[2 * pair + 1, pl.ds(first, block), :] = total[:, slots : 2 * slots]
+
+        for k in range(1, pairs + 1):
+            answer(lax.rem(my_pair + k, pairs))
+
+        def send(k, inner):
+            prof_copy(lax.rem(2 * my_pair + 2 + k, n), me, first, block).start()
+            return inner
+
+        lax.fori_loop(0, n - 2, send, 0)
+        prof_copy(4 * my_pair + 1 - me, me, first, block).start()
+        return carry
+
+    lax.fori_loop(0, padded // block, turn, 0)
+    prof_recv[me] = prof_send[me]
+
+    dot = functools.partial(jnp.dot, preferred_element_type=jnp.float32)
     for r in range(rows):
-        field_rows[:, r, :] = field[r * padded : (r + 1) * padded, :].astype(jnp.float32)
+        value = state[r]
+        high = value.astype(jnp.bfloat16)
+        low = (value - high.astype(jnp.float32)).astype(jnp.bfloat16)
+        mixed = dot(vert_hi, high) + (dot(vert_hi, low) + dot(vert_lo, high))
+        scale = edge_send[rows + r : rows + r + 1, :]
+        field[r * padded : (r + 1) * padded, :] = (mixed * scale).astype(jnp.bfloat16)
+    lane = lax.broadcasted_iota(jnp.int32, pair_shape, 0)
+    lane = jnp.where(lane < half, 2 * lane, 2 * lane - (cols - 1))
+    merge = jnp.where(lax.broadcasted_iota(jnp.int32, pair_shape, 1) == lane, 1.0, 0.0)
+    merge = merge.astype(jnp.bfloat16)
+    for r in range(rows):
+        field_rows[:, r, :] = dot(field[r * padded : (r + 1) * padded, :], merge)
     pert_ref[...] = field_rows[0:levels].astype(jnp.bfloat16)
 
-    def finish(k, carry):
+    def await_prof(k, carry):
         source = lax.rem(me + n - k, n)
-        prof_copy(source, source).wait_recv()
-        prof_ref[0, source] = prof_recv[source, 0:levels, :]
-        return carry
-
-    lax.fori_loop(1, n, finish, 0)
+        prof_copy(source, source, 0, padded).wait_recv()
+        return carry
+
+    lax.fori_loop(1, n, await_prof, 0)
+
+    both = jnp.concatenate([vert_hi, vert_lo], 0)
+    for source in range(0, n, 2):
+        arrived = jnp.concatenate([prof_recv[source], prof_recv[source + 1]], 1)
+        mixed = dot(both, arrived)
+        mixed = mixed[0:padded] + mixed[padded : 2 * padded]
+        for side in range(2):
+            live = slot_ids < count_ref[0, source + side]
+            prof_rows[:, source + side, :] = jnp.where(
+                live, mixed[:, side * slots : (side + 1) * slots], 0.0
+            )
+    prof_ref[...] = prof_rows[0:levels].astype(jnp.bfloat16)
 
     def settle(k, carry):
         peer = lax.rem(me + k, n)
         probe_copy(peer, me).wait_send()
-        prof_copy(peer, me).wait_send()
+        prof_copy(peer, me, 0, padded).wait_send()
         return carry
 
     lax.fori_loop(1, n, settle, 0)
@@ -339,11 +398,11 @@
     vmem = pl.BlockSpec(memory_space=pltpu.VMEM)
     hbm = pl.BlockSpec(memory_space=pltpu.HBM)
     dma = pltpu.SemaphoreType.DMA
-    return pl.pallas_call(
+    perturbation, profiles = pl.pallas_call(
         functools.partial(kernel, n),
         out_shape=(
             jax.ShapeDtypeStruct((levels, rows, cols), bf16),
-            jax.ShapeDtypeStruct((1, n, levels, slots), bf16),
+            jax.ShapeDtypeStruct((levels, n, slots), bf16),
         ),
         in_specs=[hbm] * 8,
         out_specs=(vmem, vmem),
@@ -367,10 +426,15 @@
             pltpu.VMEM((span, GROUP, cols), f32),
             pltpu.VMEM((span, GROUP, cols), f32),
             pltpu.VMEM((span, GROUP, cols), f32),
-            pltpu.VMEM((kept, padded, cols), f32),
+            pltpu.VMEM((kept, GROUP, cols), f32),
+            pltpu.VMEM((rows, padded, cols), f32),
             pltpu.VMEM((padded, 128), f32),
-            pltpu.VMEM((kept * padded, cols), bf16),
+            pltpu.VMEM((kept * 2 * GROUP, cols), f32),
+            pltpu.VMEM((n // 2, cols, 2 * slots), bf16),
+            pltpu.VMEM((n // 2, 2 * GROUP, 2 * slots), f32),
+            pltpu.VMEM((rows * padded, cols), bf16),
             pltpu.VMEM((padded, rows, cols), f32),
+            pltpu.VMEM((padded, n, slots), f32),
             pltpu.VMEM((n, padded, slots), bf16),
             pltpu.VMEM((n, padded, slots), bf16),
             dma((3,)),
@@ -393,6 +457,7 @@
         obs_cell,
         obs_frac,
     )
+    return (perturbation, jnp.transpose(profiles, (1, 0, 2))[None])
 
 
 def solution(mesh):

time: 36.8 us -> 29.6 us (0.80)
  Pallas kernels: 33.1 us -> 26.2 us
    pallas_call x1, Pallas kernels: 33.1 us -> 26.2 us  [body(): pl.pallas_call(functools.partial(kernel, n), out_shape=(jax.ShapeDtypeStr...]
    pallas_call x1 -> x0, local copies, waits for them, and re-layouts: 1.81 us -> none  [body(): pl.pallas_call(functools.partial(kernel, n), out_shape=(jax.ShapeDtypeStr...]
    unnamed x3 -> x4, local copies, waits for them, and re-layouts: 0.72 us -> 2.47 us
where the time goes in v3:
time: 29.6 us; the launch traced here: 29.3 us
  Pallas kernels  26.2 us (89%)
  local copies, waits for them, and re-layouts  2.47 us (8%)
  between operations  0.65 us (2%)
    pallas_call x1, Pallas kernels, body(): pl.pallas_call(functools.partial(kernel, n), out_shape=(jax.ShapeDtypeStr...  26.2 us
    unnamed x4, local copies, waits for them, and re-layouts  2.47 us

profile of v3, /device:TPU:0, one launch (start us, length us, event | category | flops | bytes accessed | tf_op | source)
XLA Modules:
  0.0 29.3 jit_solution(14207566318963412838)
XLA Ops:
  0.6 26.2 %shard_map.95 = (bf16[75,8,256]{2,1,0:T(8,128)(2,1)}, bf16[75,16,128]{2,1,0:T(8,128)(2,1)}) custom-call(s32[2]{0:T(128)} %seeds_hbm.1, s32[1,16]{1,0:T(1,128)} %count_hbm.1, f32[8,256]{1,0:T(8,128)} %diff_hbm.1, s32[8,256]{1,0:T(8,128)} %wet_hbm.1, f32[75,75]{1,0:T(8,128)} %vert_hbm.1, f32[8,256]{1,0:T(8,128)} %scale_hbm.1, s32[1,16,128]{2,1,0:T(8,128)} %cell_hbm.1, ...), custom_call_target="tpu_custom_call" | custom-call | tf_op jit(solution)/shard_map/pallas_call | solution.py:401
  26.9 0.0 copy-start
  26.9 1.7 %copy.12 = bf16[75,8,256]{2,1,0:T(8,128)(2,1)} copy(bf16[75,8,256]{2,1,0:T(8,128)(2,1)} %get-tuple-element.8) | data formatting | bytes 614400
  28.6 0.0 copy-done
  28.6 0.7 %copy.13 = bf16[1,16,75,128]{3,1,2,0:T(8,128)(2,1)} copy(bf16[1,16,75,128]{3,1,2,0:T(8,128)(2,1)S(1)} %bitcast.3) | data formatting | bytes 614400
Async XLA Ops:
  26.9 1.8 %copy-start = (bf16[75,16,128]{2,1,0:T(8,128)(2,1)S(1)}, bf16[75,16,128]{2,1,0:T(8,128)(2,1)}, u32[]{:S(2)}) copy-start(bf16[75,16,128]{2,1,0:T(8,128)(2,1)} %get-tuple-element.5) | copy-start | bytes 921604

commit v4 on v3

--- a/solution.py
+++ b/solution.py
@@ -58,7 +58,6 @@
     shares,
     field,
     field_rows,
-    prof_rows,
     prof_send,
     prof_recv,
     edge_ss,
@@ -110,55 +109,18 @@
         pull.wait()
 
     kappa = diff_ref[...] * wet_ref[...].astype(jnp.float32)
+    dot = functools.partial(jnp.dot, preferred_element_type=jnp.float32)
     pair_shape = (cols, cols)
     lane = lax.broadcasted_iota(jnp.int32, pair_shape, 1)
     lane = jnp.where(lane < half, 2 * lane, 2 * lane - (cols - 1))
     split = jnp.where(lax.broadcasted_iota(jnp.int32, pair_shape, 0) == lane, 1.0, 0.0)
-    edge_send[...] = jnp.dot(
-        jnp.concatenate([kappa, scale_ref[...]], 0),
-        split,
-        precision=lax.Precision.HIGHEST,
-        preferred_element_type=jnp.float32,
-    )
-    slot_ids = lax.broadcasted_iota(jnp.int32, (1, slots), 1)
-
-    def pack(h, carry):
-        anchor = cell_ref[0, pl.ds(h, 1), :]
-        frac = frac_ref[0, h]
-        row = lax.shift_right_logical(anchor, jnp.int32(cols.bit_length() - 1))
-        col = anchor - row * cols
-        probe_send[h, 0:1, :] = col.astype(jnp.float32)
-        probe_send[h, 1:2, :] = frac[1:2, :]
-        probe_send[h, 2:3, :] = row.astype(jnp.float32)
-        probe_send[h, 3:4, :] = frac[0:1, :]
-        probe_send[h, 4:8, :] = jnp.zeros((4, slots), jnp.float32)
-        return carry
-
-    lax.fori_loop(0, n, pack, 0)
-
-    seed_a = seeds_ref[0]
-    seed_b = seeds_ref[1]
-    shape = (GROUP, cols)
-    col_ids = lax.broadcasted_iota(jnp.int32, shape, 1)
-    col_ids = jnp.where(col_ids < half, 2 * col_ids, 2 * col_ids - (cols - 1))
-    spread_ids = (
-        lax.broadcasted_iota(jnp.int32, shape, 0) * (total_rows * cols) + col_ids
-    ) * jnp.int32(-1640531535)
-    first_row = me * rows - STEPS
-
-    def draw(g, carry):
-        at = pl.multiple_of(g * GROUP, GROUP)
-        for j in range(span):
-            base = (g * (GROUP * total_rows) + first_row + j) * cols
-            hashed = scramble(spread_ids + (base * jnp.int32(-1640531535) + seed_a))
-            hashed = scramble(hashed ^ seed_b)
-            drawn = lax.shift_right_logical(hashed, jnp.int32(8)).astype(jnp.float32)
-            noise[j, pl.ds(at, GROUP), :] = drawn * (SPREAD / 16777216.0) + SPREAD * (
-                0.5 / 16777216.0 - 0.5
-            )
-        return carry
-
-    lax.fori_loop(0, groups // 2, draw, 0)
+    plain = jnp.concatenate([kappa, scale_ref[...]], 0)
+    high = plain.astype(jnp.bfloat16)
+    rest = plain - high.astype(jnp.float32)
+    middle = rest.astype(jnp.bfloat16)
+    low = (rest - middle.astype(jnp.float32)).astype(jnp.bfloat16)
+    terms = dot(jnp.concatenate([high, middle, low], 0), split.astype(jnp.bfloat16))
+    edge_send[...] = (terms[0 : 2 * rows] + terms[2 * rows : 4 * rows]) + terms[4 * rows :]
 
     pl.semaphore_wait(barrier, n - 1)
 
@@ -191,6 +153,22 @@
     for which in range(3):
         edge_copy(which).start()
 
+    slot_ids = lax.broadcasted_iota(jnp.int32, (1, slots), 1)
+
+    def pack(h, carry):
+        anchor = cell_ref[0, pl.ds(h, 1), :]
+        frac = frac_ref[0, h]
+        row = lax.shift_right_logical(anchor, jnp.int32(cols.bit_length() - 1))
+        col = anchor - row * cols
+        probe_send[h, 0:1, :] = col.astype(jnp.float32)
+        probe_send[h, 1:2, :] = frac[1:2, :]
+        probe_send[h, 2:3, :] = row.astype(jnp.float32)
+        probe_send[h, 3:4, :] = frac[0:1, :]
+        probe_send[h, 4:8, :] = jnp.zeros((4, slots), jnp.float32)
+        return carry
+
+    lax.fori_loop(0, n, pack, 0)
+
     def send_probe(k, carry):
         probe_copy(lax.rem(me + k, n), me).start()
         return carry
@@ -198,7 +176,29 @@
     lax.fori_loop(1, n, send_probe, 0)
     probe_recv[me] = probe_send[me]
 
-    lax.fori_loop(groups // 2, groups, draw, 0)
+    seed_a = seeds_ref[0]
+    seed_b = seeds_ref[1]
+    shape = (GROUP, cols)
+    col_ids = lax.broadcasted_iota(jnp.int32, shape, 1)
+    col_ids = jnp.where(col_ids < half, 2 * col_ids, 2 * col_ids - (cols - 1))
+    spread_ids = (
+        lax.broadcasted_iota(jnp.int32, shape, 0) * (total_rows * cols) + col_ids
+    ) * jnp.int32(-1640531535)
+    first_row = me * rows - STEPS
+
+    def draw(g, carry):
+        at = pl.multiple_of(g * GROUP, GROUP)
+        for j in range(span):
+            base = (g * (GROUP * total_rows) + first_row + j) * cols
+            hashed = scramble(spread_ids + (base * jnp.int32(-1640531535) + seed_a))
+            hashed = scramble(hashed ^ seed_b)
+            drawn = lax.shift_right_logical(hashed, jnp.int32(8)).astype(jnp.float32)
+            noise[j, pl.ds(at, GROUP), :] = drawn * (SPREAD / 16777216.0) + SPREAD * (
+                0.5 / 16777216.0 - 0.5
+            )
+        return carry
+
+    lax.fori_loop(0, groups, draw, 0)
 
     vert_pad[...] = jnp.zeros_like(vert_pad)
     vert_pad[0:levels, 0:levels] = vert_ref[...]
@@ -297,23 +297,12 @@
 
     block = 2 * GROUP
     my_pair = me // 2
-
-    def turn(b, carry):
-        first = pl.multiple_of(b * block, block)
-        for part in range(2):
-            at = pl.multiple_of(first + part * GROUP, GROUP)
-            evens, odds = advance(at)
-            for r in range(kept):
-                if r < rows:
-                    state[r, pl.ds(at, GROUP), 0:half] = evens[r]
-                    state[r, pl.ds(at, GROUP), half:cols] = odds[r]
-                line = r * block + part * GROUP
-                scaled[line : line + GROUP, 0:half] = evens[r] * scale_all[r, :, 0:half]
-                scaled[line : line + GROUP, half:cols] = odds[r] * scale_all[r, :, half:cols]
-        left = scaled[...].astype(jnp.bfloat16)
-
-        def answer(pair):
-            across = jnp.dot(left, weights[pair], preferred_element_type=jnp.float32)
+    some = pairs // 2
+
+    def answer(left, first, side):
+        for q in range(some):
+            pair = lax.rem(my_pair + 1 + side * some + q, pairs)
+            across = dot(left, weights[pair])
             total = None
             for r in range(kept):
                 term = across[r * block : (r + 1) * block] * shares[pair, r : r + 1, :]
@@ -322,21 +311,47 @@
             prof_send[2 * pair, pl.ds(first, block), :] = total[:, 0:slots]
             prof_send[2 * pair + 1, pl.ds(first, block), :] = total[:, slots : 2 * slots]
 
-        for k in range(1, pairs + 1):
-            answer(lax.rem(my_pair + k, pairs))
-
-        def send(k, inner):
-            prof_copy(lax.rem(2 * my_pair + 2 + k, n), me, first, block).start()
-            return inner
-
-        lax.fori_loop(0, n - 2, send, 0)
-        prof_copy(4 * my_pair + 1 - me, me, first, block).start()
-        return carry
-
-    lax.fori_loop(0, padded // block, turn, 0)
+    def send(ready, first, side):
+        for k in range(2 * some):
+            peer = lax.rem(2 * (my_pair + 1 + side * some) + k, n)
+
+            @pl.when(jnp.logical_and(ready, peer != me))
+            def _():
+                prof_copy(peer, me, first, block).start()
+
+    def left_of(slot):
+        return scaled[slot].reshape(kept * block, cols).astype(jnp.bfloat16)
+
+    def turn(g, carry):
+        at = pl.multiple_of(g * GROUP, GROUP)
+        side = lax.rem(g, 2)
+        slot = lax.rem(g // 2, 2)
+        before = pl.multiple_of(jnp.maximum(g // 2 - 1, 0) * block, block)
+        answer(left_of(1 - slot), before, side)
+        evens, odds = advance(at)
+        line = pl.multiple_of(side * GROUP, GROUP)
+        for r in range(kept):
+            if r < rows:
+                state[r, pl.ds(at, GROUP), 0:half] = evens[r]
+                state[r, pl.ds(at, GROUP), half:cols] = odds[r]
+            scaled[slot, r, pl.ds(line, GROUP), 0:half] = evens[r] * scale_all[r, :, 0:half]
+            scaled[slot, r, pl.ds(line, GROUP), half:cols] = (
+                odds[r] * scale_all[r, :, half:cols]
+            )
+        send(g >= 2, before, side)
+        return carry
+
+    scaled[1] = jnp.zeros((kept, block, cols), jnp.float32)
+    lax.fori_loop(0, groups, turn, 0)
+
+    def last_turn(side, carry):
+        answer(left_of((groups // 2 - 1) % 2), padded - block, side)
+        send(side >= 0, padded - block, side)
+        return carry
+
+    lax.fori_loop(0, 2, last_turn, 0)
     prof_recv[me] = prof_send[me]
 
-    dot = functools.partial(jnp.dot, preferred_element_type=jnp.float32)
     for r in range(rows):
         value = state[r]
         high = value.astype(jnp.bfloat16)
@@ -366,10 +381,8 @@
         mixed = mixed[0:padded] + mixed[padded : 2 * padded]
         for side in range(2):
             live = slot_ids < count_ref[0, source + side]
-            prof_rows[:, source + side, :] = jnp.where(
-                live, mixed[:, side * slots : (side + 1) * slots], 0.0
-            )
-    prof_ref[...] = prof_rows[0:levels].astype(jnp.bfloat16)
+            mine = mixed[0:levels, side * slots : (side + 1) * slots]
+            prof_ref[0, source + side] = jnp.where(live, mine, 0.0).astype(jnp.bfloat16)
 
     def settle(k, carry):
         peer = lax.rem(me + k, n)
@@ -389,7 +402,7 @@
     levels = vert_factor.shape[0]
     n = lax.axis_size("tile")
     slots = obs_cell.shape[2]
-    if rows != STEPS or n % 2 or cols & (cols - 1):
+    if rows != STEPS or n % 4 or cols & (cols - 1):
         raise ValueError("unsupported sizes")
     padded = -(-levels // 16) * 16
     span = rows + 2 * STEPS + 1
@@ -398,11 +411,11 @@
     vmem = pl.BlockSpec(memory_space=pltpu.VMEM)
     hbm = pl.BlockSpec(memory_space=pltpu.HBM)
     dma = pltpu.SemaphoreType.DMA
-    perturbation, profiles = pl.pallas_call(
+    return pl.pallas_call(
         functools.partial(kernel, n),
         out_shape=(
             jax.ShapeDtypeStruct((levels, rows, cols), bf16),
-            jax.ShapeDtypeStruct((levels, n, slots), bf16),
+            jax.ShapeDtypeStruct((1, n, levels, slots), bf16),
         ),
         in_specs=[hbm] * 8,
         out_specs=(vmem, vmem),
@@ -429,12 +442,11 @@
             pltpu.VMEM((kept, GROUP, cols), f32),
             pltpu.VMEM((rows, padded, cols), f32),
             pltpu.VMEM((padded, 128), f32),
-            pltpu.VMEM((kept * 2 * GROUP, cols), f32),
+            pltpu.VMEM((2, kept, 2 * GROUP, cols), f32),
             pltpu.VMEM((n // 2, cols, 2 * slots), bf16),
             pltpu.VMEM((n // 2, 2 * GROUP, 2 * slots), f32),
             pltpu.VMEM((rows * padded, cols), bf16),
             pltpu.VMEM((padded, rows, cols), f32),
-            pltpu.VMEM((padded, n, slots), f32),
             pltpu.VMEM((n, padded, slots), bf16),
             pltpu.VMEM((n, padded, slots), bf16),
             dma((3,)),
@@ -457,7 +469,6 @@
         obs_cell,
         obs_frac,
     )
-    return (perturbation, jnp.transpose(profiles, (1, 0, 2))[None])
 
 
 def solution(mesh):

time: 29.6 us -> 33.4 us (1.13)
  Pallas kernels: 26.2 us -> 30 us
    pallas_call x1, Pallas kernels: 26.2 us -> 30 us  [body(): pl.pallas_call(functools.partial(kernel, n), out_shape=(jax.ShapeDtypeStr...]
    pallas_call x0 -> x1, local copies, waits for them, and re-layouts: none -> 1.81 us  [body(): pl.pallas_call(functools.partial(kernel, n), out_shape=(jax.ShapeDtypeStr...]
    unnamed x4 -> x3, local copies, waits for them, and re-layouts: 2.47 us -> 0.72 us
where the time goes in v4:
time: 33.4 us; the launch traced here: 33.2 us
  Pallas kernels  30 us (90%)
  local copies, waits for them, and re-layouts  2.54 us (8%)
  between operations  0.65 us (2%)
    pallas_call x1, Pallas kernels, body(): pl.pallas_call(functools.partial(kernel, n), out_shape=(jax.ShapeDtypeStr...  30 us
    pallas_call x1, local copies, waits for them, and re-layouts, body(): pl.pallas_call(functools.partial(kernel, n), out_shape=(jax.ShapeDtypeStr...  1.81 us
    unnamed x3, local copies, waits for them, and re-layouts  0.72 us

profile of v4, /device:TPU:0, one launch (start us, length us, event | category | flops | bytes accessed | tf_op | source)
XLA Modules:
  0.0 33.2 jit_solution(2633349111950586118)
XLA Ops:
  0.6 30.0 %shard_map.95 = (bf16[75,8,256]{2,1,0:T(8,128)(2,1)}, bf16[1,16,75,128]{3,2,1,0:T(8,128)(2,1)}) custom-call(s32[2]{0:T(128)} %seeds_hbm.1, s32[1,16]{1,0:T(1,128)} %count_hbm.1, f32[8,256]{1,0:T(8,128)} %diff_hbm.1, s32[8,256]{1,0:T(8,128)} %wet_hbm.1, f32[75,75]{1,0:T(8,128)} %vert_hbm.1, f32[8,256]{1,0:T(8,128)} %scale_hbm.1, s32[1,16,128]{2,1,0:T(8,128)} %cell_hbm.1, ...), custom_call_target="tpu_custom_call" | custom-call | tf_op jit(solution)/shard_map/pallas_call | solution.py:414
  30.7 0.0 copy-start
  30.7 1.8 %copy.10 = bf16[1,16,75,128]{3,1,2,0:T(8,128)(2,1)} copy(bf16[1,16,75,128]{3,2,1,0:T(8,128)(2,1)} %get-tuple-element.3) | data formatting | bytes 614400 | tf_op jit(solution)/shard_map/pallas_call | solution.py:414
  32.5 0.0 copy-done
  32.5 0.7 %copy.12 = bf16[75,8,256]{2,1,0:T(8,128)(2,1)} copy(bf16[75,8,256]{2,1,0:T(8,128)(2,1)S(1)} %copy-done) | data formatting | bytes 614400
Async XLA Ops:
  30.7 1.8 %copy-start = (bf16[75,8,256]{2,1,0:T(8,128)(2,1)S(1)}, bf16[75,8,256]{2,1,0:T(8,128)(2,1)}, u32[]{:S(2)}) copy-start(bf16[75,8,256]{2,1,0:T(8,128)(2,1)} %get-tuple-element.6) | copy-start | bytes 921604

commit v5 on v3

--- a/solution.py
+++ b/solution.py
@@ -47,6 +47,7 @@
     probe_send,
     probe_recv,
     noise,
+    work,
     face_rows,
     face_cols,
     wet_all,
@@ -58,7 +59,6 @@
     shares,
     field,
     field_rows,
-    prof_rows,
     prof_send,
     prof_recv,
     edge_ss,
@@ -114,12 +114,14 @@
     lane = lax.broadcasted_iota(jnp.int32, pair_shape, 1)
     lane = jnp.where(lane < half, 2 * lane, 2 * lane - (cols - 1))
     split = jnp.where(lax.broadcasted_iota(jnp.int32, pair_shape, 0) == lane, 1.0, 0.0)
-    edge_send[...] = jnp.dot(
-        jnp.concatenate([kappa, scale_ref[...]], 0),
-        split,
-        precision=lax.Precision.HIGHEST,
-        preferred_element_type=jnp.float32,
-    )
+    plain = jnp.concatenate([kappa, scale_ref[...]], 0)
+    high = plain.astype(jnp.bfloat16)
+    rest = plain - high.astype(jnp.float32)
+    middle = rest.astype(jnp.bfloat16)
+    low = (rest - middle.astype(jnp.float32)).astype(jnp.bfloat16)
+    dot = functools.partial(jnp.dot, preferred_element_type=jnp.float32)
+    terms = dot(jnp.concatenate([high, middle, low], 0), split.astype(jnp.bfloat16))
+    edge_send[...] = (terms[0 : 2 * rows] + terms[2 * rows : 4 * rows]) + terms[4 * rows :]
     slot_ids = lax.broadcasted_iota(jnp.int32, (1, slots), 1)
 
     def pack(h, carry):
@@ -265,25 +267,26 @@
         def take(ref, j, lo):
             return ref[j, :, lo : lo + half]
 
-        old_e, old_o = [], []
         for j in range(span):
-            old_e.append(noise[j, pl.ds(at, GROUP), 0:half] * take(wet_all, j, 0))
-            old_o.append(noise[j, pl.ds(at, GROUP), half:cols] * take(wet_all, j, half))
+            work[j] = noise[j, pl.ds(at, GROUP), :] * wet_all[j]
         for step in range(STEPS):
-            new_e, new_o = list(old_e), list(old_o)
-            up_e = take(face_rows, step, 0) * (old_e[step + 1] - old_e[step])
-            up_o = take(face_rows, step, half) * (old_o[step + 1] - old_o[step])
-            for j in range(step + 1, span - 1 - step):
-                here_e, here_o = old_e[j], old_o[j]
-                down_e = take(face_rows, j, 0) * (old_e[j + 1] - here_e)
-                down_o = take(face_rows, j, half) * (old_o[j + 1] - here_o)
-                inner = take(face_cols, j, 0) * (here_o - here_e)
-                outer = take(face_cols, j, half) * (pltpu.roll(here_e, half - 1, 1) - here_o)
-                new_e[j] = here_e + ((down_e - up_e) + (inner - pltpu.roll(outer, 1, 1)))
-                new_o[j] = here_o + ((down_o - up_o) + (outer - inner))
+            here_e, here_o = take(work, step, 0), take(work, step, half)
+            up_e = up_o = None
+            for j in range(step, span - 1 - step):
+                next_e, next_o = take(work, j + 1, 0), take(work, j + 1, half)
+                down_e = take(face_rows, j, 0) * (next_e - here_e)
+                down_o = take(face_rows, j, half) * (next_o - here_o)
+                if j > step:
+                    inner = take(face_cols, j, 0) * (here_o - here_e)
+                    outer = take(face_cols, j, half) * (
+                        pltpu.roll(here_e, half - 1, 1) - here_o
+                    )
+                    work[j, :, 0:half] = here_e + (
+                        (down_e - up_e) + (inner - pltpu.roll(outer, 1, 1))
+                    )
+                    work[j, :, half:cols] = here_o + ((down_o - up_o) + (outer - inner))
                 up_e, up_o = down_e, down_o
-            old_e, old_o = new_e, new_o
-        return old_e[STEPS : STEPS + kept], old_o[STEPS : STEPS + kept]
+                here_e, here_o = next_e, next_o
 
     def prof_copy(peer, slot, at, size):
         return pltpu.make_async_remote_copy(
@@ -300,17 +303,20 @@
 
     def turn(b, carry):
         first = pl.multiple_of(b * block, block)
-        for part in range(2):
+
+        def grow(part, inner):
             at = pl.multiple_of(first + part * GROUP, GROUP)
-            evens, odds = advance(at)
+            line = pl.multiple_of(part * GROUP, GROUP)
+            advance(at)
             for r in range(kept):
+                value = work[STEPS + r]
                 if r < rows:
-                    state[r, pl.ds(at, GROUP), 0:half] = evens[r]
-                    state[r, pl.ds(at, GROUP), half:cols] = odds[r]
-                line = r * block + part * GROUP
-                scaled[line : line + GROUP, 0:half] = evens[r] * scale_all[r, :, 0:half]
-                scaled[line : line + GROUP, half:cols] = odds[r] * scale_all[r, :, half:cols]
-        left = scaled[...].astype(jnp.bfloat16)
+                    state[r, pl.ds(at, GROUP), :] = value
+                scaled[r, pl.ds(line, GROUP), :] = value * scale_all[r]
+            return inner
+
+        lax.fori_loop(0, 2, grow, 0)
+        left = scaled[...].reshape(kept * block, cols).astype(jnp.bfloat16)
 
         def answer(pair):
             across = jnp.dot(left, weights[pair], preferred_element_type=jnp.float32)
@@ -336,7 +342,6 @@
     lax.fori_loop(0, padded // block, turn, 0)
     prof_recv[me] = prof_send[me]
 
-    dot = functools.partial(jnp.dot, preferred_element_type=jnp.float32)
     for r in range(rows):
         value = state[r]
         high = value.astype(jnp.bfloat16)
@@ -366,10 +371,8 @@
         mixed = mixed[0:padded] + mixed[padded : 2 * padded]
         for side in range(2):
             live = slot_ids < count_ref[0, source + side]
-            prof_rows[:, source + side, :] = jnp.where(
-                live, mixed[:, side * slots : (side + 1) * slots], 0.0
-            )
-    prof_ref[...] = prof_rows[0:levels].astype(jnp.bfloat16)
+            mine = mixed[0:levels, side * slots : (side + 1) * slots]
+            prof_ref[0, source + side] = jnp.where(live, mine, 0.0).astype(jnp.bfloat16)
 
     def settle(k, carry):
         peer = lax.rem(me + k, n)
@@ -398,11 +401,11 @@
     vmem = pl.BlockSpec(memory_space=pltpu.VMEM)
     hbm = pl.BlockSpec(memory_space=pltpu.HBM)
     dma = pltpu.SemaphoreType.DMA
-    perturbation, profiles = pl.pallas_call(
+    return pl.pallas_call(
         functools.partial(kernel, n),
         out_shape=(
             jax.ShapeDtypeStruct((levels, rows, cols), bf16),
-            jax.ShapeDtypeStruct((levels, n, slots), bf16),
+            jax.ShapeDtypeStruct((1, n, levels, slots), bf16),
         ),
         in_specs=[hbm] * 8,
         out_specs=(vmem, vmem),
@@ -426,15 +429,15 @@
             pltpu.VMEM((span, GROUP, cols), f32),
             pltpu.VMEM((span, GROUP, cols), f32),
             pltpu.VMEM((span, GROUP, cols), f32),
+            pltpu.VMEM((span, GROUP, cols), f32),
             pltpu.VMEM((kept, GROUP, cols), f32),
             pltpu.VMEM((rows, padded, cols), f32),
             pltpu.VMEM((padded, 128), f32),
-            pltpu.VMEM((kept * 2 * GROUP, cols), f32),
+            pltpu.VMEM((kept, 2 * GROUP, cols), f32),
             pltpu.VMEM((n // 2, cols, 2 * slots), bf16),
             pltpu.VMEM((n // 2, 2 * GROUP, 2 * slots), f32),
             pltpu.VMEM((rows * padded, cols), bf16),
             pltpu.VMEM((padded, rows, cols), f32),
-            pltpu.VMEM((padded, n, slots), f32),
             pltpu.VMEM((n, padded, slots), bf16),
             pltpu.VMEM((n, padded, slots), bf16),
             dma((3,)),
@@ -457,7 +460,6 @@
         obs_cell,
         obs_frac,
     )
-    return (perturbation, jnp.transpose(profiles, (1, 0, 2))[None])
 
 
 def solution(mesh):

time: 29.6 us -> 34.6 us (1.17)
  Pallas kernels: 26.2 us -> 31.3 us
    pallas_call x1, Pallas kernels: 26.2 us -> 31.3 us  [body(): pl.pallas_call(functools.partial(kernel, n), out_shape=(jax.ShapeDtypeStr...]
    pallas_call x0 -> x1, local copies, waits for them, and re-layouts: none -> 1.81 us  [body(): pl.pallas_call(functools.partial(kernel, n), out_shape=(jax.ShapeDtypeStr...]
    unnamed x4 -> x3, local copies, waits for them, and re-layouts: 2.47 us -> 0.72 us
where the time goes in v5:
time: 34.6 us; the launch traced here: 34.4 us
  Pallas kernels  31.3 us (90%)
  local copies, waits for them, and re-layouts  2.54 us (7%)
  between operations  0.65 us (2%)
    pallas_call x1, Pallas kernels, body(): pl.pallas_call(functools.partial(kernel, n), out_shape=(jax.ShapeDtypeStr...  31.3 us
    pallas_call x1, local copies, waits for them, and re-layouts, body(): pl.pallas_call(functools.partial(kernel, n), out_shape=(jax.ShapeDtypeStr...  1.81 us
    unnamed x3, local copies, waits for them, and re-layouts  0.72 us

profile of v5, /device:TPU:0, one launch (start us, length us, event | category | flops | bytes accessed | tf_op | source)
XLA Modules:
  0.0 34.4 jit_solution(15041463380154952418)
XLA Ops:
  0.6 31.3 %shard_map.95 = (bf16[75,8,256]{2,1,0:T(8,128)(2,1)}, bf16[1,16,75,128]{3,2,1,0:T(8,128)(2,1)}) custom-call(s32[2]{0:T(128)} %seeds_hbm.1, s32[1,16]{1,0:T(1,128)} %count_hbm.1, f32[8,256]{1,0:T(8,128)} %diff_hbm.1, s32[8,256]{1,0:T(8,128)} %wet_hbm.1, f32[75,75]{1,0:T(8,128)} %vert_hbm.1, f32[8,256]{1,0:T(8,128)} %scale_hbm.1, s32[1,16,128]{2,1,0:T(8,128)} %cell_hbm.1, ...), custom_call_target="tpu_custom_call" | custom-call | tf_op jit(solution)/shard_map/pallas_call | solution.py:404
  31.9 0.0 copy-start
  31.9 1.8 %copy.10 = bf16[1,16,75,128]{3,1,2,0:T(8,128)(2,1)} copy(bf16[1,16,75,128]{3,2,1,0:T(8,128)(2,1)} %get-tuple-element.3) | data formatting | bytes 614400 | tf_op jit(solution)/shard_map/pallas_call | solution.py:404
  33.7 0.0 copy-done
  33.7 0.7 %copy.12 = bf16[75,8,256]{2,1,0:T(8,128)(2,1)} copy(bf16[75,8,256]{2,1,0:T(8,128)(2,1)S(1)} %copy-done) | data formatting | bytes 614400
Async XLA Ops:
  31.9 1.8 %copy-start = (bf16[75,8,256]{2,1,0:T(8,128)(2,1)S(1)}, bf16[75,8,256]{2,1,0:T(8,128)(2,1)}, u32[]{:S(2)}) copy-start(bf16[75,8,256]{2,1,0:T(8,128)(2,1)} %get-tuple-element.6) | copy-start | bytes 921604

commit v6 on v5

--- a/solution.py
+++ b/solution.py
@@ -50,6 +50,7 @@
     work,
     face_rows,
     face_cols,
+    face_left,
     wet_all,
     scale_all,
     state,
@@ -227,10 +228,12 @@
     faces_in = jnp.sqrt(even * odd)
     faces_out = jnp.where(last, 0.0, jnp.sqrt(odd * pltpu.roll(even, half - 1, 1)))
     faces_c = jnp.concatenate([faces_in, faces_out], 1)
+    faces_left = pltpu.roll(faces_out, 1, 1)
     faces_r = jnp.sqrt(kappa_all[0 : span - 1] * kappa_all[1:span])
     for j in range(span):
         wet_all[j] = jnp.broadcast_to(wet[j : j + 1], shape)
         face_cols[j] = jnp.broadcast_to(faces_c[j : j + 1], shape)
+        face_left[j] = jnp.broadcast_to(faces_left[j : j + 1], (GROUP, half))
         if j < span - 1:
             face_rows[j] = jnp.broadcast_to(faces_r[j : j + 1], shape)
     for r in range(kept):
@@ -263,30 +266,40 @@
 
     lax.fori_loop(0, pairs, weigh, 0)
 
-    def advance(at):
+    def advance(first):
         def take(ref, j, lo):
             return ref[j, :, lo : lo + half]
 
+        parts = [pl.ds(part * GROUP, GROUP) for part in range(2)]
         for j in range(span):
-            work[j] = noise[j, pl.ds(at, GROUP), :] * wet_all[j]
+            for part in range(2):
+                at = pl.multiple_of(first + part * GROUP, GROUP)
+                work[j, parts[part], :] = noise[j, pl.ds(at, GROUP), :] * wet_all[j]
         for step in range(STEPS):
-            here_e, here_o = take(work, step, 0), take(work, step, half)
-            up_e = up_o = None
+            here = [
+                (work[step, part, 0:half], work[step, part, half:cols]) for part in parts
+            ]
+            up = [None, None]
             for j in range(step, span - 1 - step):
-                next_e, next_o = take(work, j + 1, 0), take(work, j + 1, half)
-                down_e = take(face_rows, j, 0) * (next_e - here_e)
-                down_o = take(face_rows, j, half) * (next_o - here_o)
+                rows_e, rows_o = take(face_rows, j, 0), take(face_rows, j, half)
                 if j > step:
-                    inner = take(face_cols, j, 0) * (here_o - here_e)
-                    outer = take(face_cols, j, half) * (
-                        pltpu.roll(here_e, half - 1, 1) - here_o
-                    )
-                    work[j, :, 0:half] = here_e + (
-                        (down_e - up_e) + (inner - pltpu.roll(outer, 1, 1))
-                    )
-                    work[j, :, half:cols] = here_o + ((down_o - up_o) + (outer - inner))
-                up_e, up_o = down_e, down_o
-                here_e, here_o = next_e, next_o
+                    cols_in = take(face_cols, j, 0)
+                    cols_right = take(face_cols, j, half)
+                    cols_left = face_left[j]
+                for k, part in enumerate(parts):
+                    here_e, here_o = here[k]
+                    next_e, next_o = work[j + 1, part, 0:half], work[j + 1, part, half:cols]
+                    down_e = rows_e * (next_e - here_e)
+                    down_o = rows_o * (next_o - here_o)
+                    if j > step:
+                        up_e, up_o = up[k]
+                        inner = cols_in * (here_o - here_e)
+                        right = cols_right * (pltpu.roll(here_e, half - 1, 1) - here_o)
+                        left = cols_left * (here_e - pltpu.roll(here_o, 1, 1))
+                        work[j, part, 0:half] = here_e + ((down_e - up_e) + (inner - left))
+                        work[j, part, half:cols] = here_o + ((down_o - up_o) + (right - inner))
+                    up[k] = (down_e, down_o)
+                    here[k] = (next_e, next_o)
 
     def prof_copy(peer, slot, at, size):
         return pltpu.make_async_remote_copy(
@@ -304,18 +317,15 @@
     def turn(b, carry):
         first = pl.multiple_of(b * block, block)
 
-        def grow(part, inner):
-            at = pl.multiple_of(first + part * GROUP, GROUP)
-            line = pl.multiple_of(part * GROUP, GROUP)
-            advance(at)
-            for r in range(kept):
-                value = work[STEPS + r]
+        advance(first)
+        for r in range(kept):
+            for part in range(2):
+                here = pl.ds(part * GROUP, GROUP)
+                value = work[STEPS + r, here, :]
                 if r < rows:
+                    at = pl.multiple_of(first + part * GROUP, GROUP)
                     state[r, pl.ds(at, GROUP), :] = value
-                scaled[r, pl.ds(line, GROUP), :] = value * scale_all[r]
-            return inner
-
-        lax.fori_loop(0, 2, grow, 0)
+                scaled[r, here, :] = value * scale_all[r]
         left = scaled[...].reshape(kept * block, cols).astype(jnp.bfloat16)
 
         def answer(pair):
@@ -426,9 +436,10 @@
             pltpu.VMEM((n, 8, slots), f32),
             pltpu.VMEM((n, 8, slots), f32),
             pltpu.VMEM((span, padded, cols), f32),
+            pltpu.VMEM((span, 2 * GROUP, cols), f32),
             pltpu.VMEM((span, GROUP, cols), f32),
             pltpu.VMEM((span, GROUP, cols), f32),
-            pltpu.VMEM((span, GROUP, cols), f32),
+            pltpu.VMEM((span, GROUP, cols // 2), f32),
             pltpu.VMEM((span, GROUP, cols), f32),
             pltpu.VMEM((kept, GROUP, cols), f32),
             pltpu.VMEM((rows, padded, cols), f32),

time: 34.6 us -> 26.8 us (0.77)
  Pallas kernels: 31.3 us -> 23.4 us
    pallas_call x1, Pallas kernels: 31.3 us -> 23.4 us  [body(): pl.pallas_call(functools.partial(kernel, n), out_shape=(jax.ShapeDtypeStr...]
where the time goes in v6:
time: 26.8 us; the launch traced here: 26.6 us
  Pallas kernels  23.4 us (87%)
  local copies, waits for them, and re-layouts  2.54 us (9%)
  between operations  0.65 us (2%)
    pallas_call x1, Pallas kernels, body(): pl.pallas_call(functools.partial(kernel, n), out_shape=(jax.ShapeDtypeStr...  23.4 us
    pallas_call x1, local copies, waits for them, and re-layouts, body(): pl.pallas_call(functools.partial(kernel, n), out_shape=(jax.ShapeDtypeStr...  1.81 us
    unnamed x3, local copies, waits for them, and re-layouts  0.72 us

profile of v6, /device:TPU:0, one launch (start us, length us, event | category | flops | bytes accessed | tf_op | source)
XLA Modules:
  0.0 26.6 jit_solution(10594279559637668262)
XLA Ops:
  0.6 23.4 %shard_map.95 = (bf16[75,8,256]{2,1,0:T(8,128)(2,1)}, bf16[1,16,75,128]{3,2,1,0:T(8,128)(2,1)}) custom-call(s32[2]{0:T(128)} %seeds_hbm.1, s32[1,16]{1,0:T(1,128)} %count_hbm.1, f32[8,256]{1,0:T(8,128)} %diff_hbm.1, s32[8,256]{1,0:T(8,128)} %wet_hbm.1, f32[75,75]{1,0:T(8,128)} %vert_hbm.1, f32[8,256]{1,0:T(8,128)} %scale_hbm.1, s32[1,16,128]{2,1,0:T(8,128)} %cell_hbm.1, ...), custom_call_target="tpu_custom_call" | custom-call | tf_op jit(solution)/shard_map/pallas_call | solution.py:414
  24.1 0.0 copy-start
  24.1 1.8 %copy.10 = bf16[1,16,75,128]{3,1,2,0:T(8,128)(2,1)} copy(bf16[1,16,75,128]{3,2,1,0:T(8,128)(2,1)} %get-tuple-element.3) | data formatting | bytes 614400 | tf_op jit(solution)/shard_map/pallas_call | solution.py:414
  25.9 0.0 copy-done
  25.9 0.7 %copy.12 = bf16[75,8,256]{2,1,0:T(8,128)(2,1)} copy(bf16[75,8,256]{2,1,0:T(8,128)(2,1)S(1)} %copy-done) | data formatting | bytes 614400
Async XLA Ops:
  24.1 1.8 %copy-start = (bf16[75,8,256]{2,1,0:T(8,128)(2,1)S(1)}, bf16[75,8,256]{2,1,0:T(8,128)(2,1)}, u32[]{:S(2)}) copy-start(bf16[75,8,256]{2,1,0:T(8,128)(2,1)} %get-tuple-element.6) | copy-start | bytes 921604

commit v7 on v6

--- a/solution.py
+++ b/solution.py
@@ -73,10 +73,10 @@
         pltpu.make_async_copy(src, dst, in_sems.at[k])
         for k, (src, dst) in enumerate(
             (
+                (seeds_hbm, seeds_ref),
                 (diff_hbm, diff_ref),
                 (wet_hbm, wet_ref),
                 (scale_hbm, scale_ref),
-                (seeds_hbm, seeds_ref),
                 (count_hbm, count_ref),
                 (cell_hbm, cell_ref),
                 (frac_hbm, frac_ref),
@@ -107,7 +107,32 @@
 
     lax.fori_loop(1, n, greet, 0)
 
-    for pull in pulls:
+    pulls[0].wait()
+    seed_a = seeds_ref[0]
+    seed_b = seeds_ref[1]
+    shape = (GROUP, cols)
+    col_ids = lax.broadcasted_iota(jnp.int32, shape, 1)
+    col_ids = jnp.where(col_ids < half, 2 * col_ids, 2 * col_ids - (cols - 1))
+    spread_ids = (
+        lax.broadcasted_iota(jnp.int32, shape, 0) * (total_rows * cols) + col_ids
+    ) * jnp.int32(-1640531535)
+    first_row = me * rows - STEPS
+
+    def draw(g, carry):
+        at = pl.multiple_of(g * GROUP, GROUP)
+        for j in range(span):
+            base = (g * (GROUP * total_rows) + first_row + j) * cols
+            hashed = scramble(spread_ids + (base * jnp.int32(-1640531535) + seed_a))
+            hashed = scramble(hashed ^ seed_b)
+            drawn = lax.shift_right_logical(hashed, jnp.int32(8)).astype(jnp.float32)
+            noise[j, pl.ds(at, GROUP), :] = drawn * (SPREAD / 16777216.0) + SPREAD * (
+                0.5 / 16777216.0 - 0.5
+            )
+        return carry
+
+    lax.fori_loop(0, groups // 2, draw, 0)
+
+    for pull in pulls[1:]:
         pull.wait()
 
     kappa = diff_ref[...] * wet_ref[...].astype(jnp.float32)
@@ -125,43 +150,14 @@
     edge_send[...] = (terms[0 : 2 * rows] + terms[2 * rows : 4 * rows]) + terms[4 * rows :]
     slot_ids = lax.broadcasted_iota(jnp.int32, (1, slots), 1)
 
-    def pack(h, carry):
-        anchor = cell_ref[0, pl.ds(h, 1), :]
-        frac = frac_ref[0, h]
-        row = lax.shift_right_logical(anchor, jnp.int32(cols.bit_length() - 1))
-        col = anchor - row * cols
-        probe_send[h, 0:1, :] = col.astype(jnp.float32)
-        probe_send[h, 1:2, :] = frac[1:2, :]
-        probe_send[h, 2:3, :] = row.astype(jnp.float32)
-        probe_send[h, 3:4, :] = frac[0:1, :]
-        probe_send[h, 4:8, :] = jnp.zeros((4, slots), jnp.float32)
-        return carry
-
-    lax.fori_loop(0, n, pack, 0)
-
-    seed_a = seeds_ref[0]
-    seed_b = seeds_ref[1]
-    shape = (GROUP, cols)
-    col_ids = lax.broadcasted_iota(jnp.int32, shape, 1)
-    col_ids = jnp.where(col_ids < half, 2 * col_ids, 2 * col_ids - (cols - 1))
-    spread_ids = (
-        lax.broadcasted_iota(jnp.int32, shape, 0) * (total_rows * cols) + col_ids
-    ) * jnp.int32(-1640531535)
-    first_row = me * rows - STEPS
-
-    def draw(g, carry):
-        at = pl.multiple_of(g * GROUP, GROUP)
-        for j in range(span):
-            base = (g * (GROUP * total_rows) + first_row + j) * cols
-            hashed = scramble(spread_ids + (base * jnp.int32(-1640531535) + seed_a))
-            hashed = scramble(hashed ^ seed_b)
-            drawn = lax.shift_right_logical(hashed, jnp.int32(8)).astype(jnp.float32)
-            noise[j, pl.ds(at, GROUP), :] = drawn * (SPREAD / 16777216.0) + SPREAD * (
-                0.5 / 16777216.0 - 0.5
-            )
-        return carry
-
-    lax.fori_loop(0, groups // 2, draw, 0)
+    anchor = cell_ref[0]
+    row = lax.shift_right_logical(anchor, jnp.int32(cols.bit_length() - 1))
+    probe_send[:, 0, :] = (anchor - row * cols).astype(jnp.float32)
+    probe_send[:, 1, :] = frac_ref[0, :, 1, :]
+    probe_send[:, 2, :] = row.astype(jnp.float32)
+    probe_send[:, 3, :] = frac_ref[0, :, 0, :]
+    for k in range(4, 8):
+        probe_send[:, k, :] = jnp.zeros(anchor.shape, jnp.float32)
 
     pl.semaphore_wait(barrier, n - 1)
 
@@ -341,11 +337,8 @@
         for k in range(1, pairs + 1):
             answer(lax.rem(my_pair + k, pairs))
 
-        def send(k, inner):
+        for k in range(n - 2):
             prof_copy(lax.rem(2 * my_pair + 2 + k, n), me, first, block).start()
-            return inner
-
-        lax.fori_loop(0, n - 2, send, 0)
         prof_copy(4 * my_pair + 1 - me, me, first, block).start()
         return carry
 

time: 26.8 us -> 27 us (level)
  Pallas kernels: 23.4 us -> 23.7 us
where the time goes in v7:
time: 27 us; the launch traced here: 26.9 us
  Pallas kernels  23.7 us (88%)
  local copies, waits for them, and re-layouts  2.54 us (9%)
  between operations  0.65 us (2%)
    pallas_call x1, Pallas kernels, body(): pl.pallas_call(functools.partial(kernel, n), out_shape=(jax.ShapeDtypeStr...  23.7 us
    pallas_call x1, local copies, waits for them, and re-layouts, body(): pl.pallas_call(functools.partial(kernel, n), out_shape=(jax.ShapeDtypeStr...  1.81 us
    unnamed x3, local copies, waits for them, and re-layouts  0.72 us

profile of v7, /device:TPU:0, one launch (start us, length us, event | category | flops | bytes accessed | tf_op | source)
XLA Modules:
  0.0 26.9 jit_solution(2842970676134484323)
XLA Ops:
  0.6 23.7 %shard_map.95 = (bf16[75,8,256]{2,1,0:T(8,128)(2,1)}, bf16[1,16,75,128]{3,2,1,0:T(8,128)(2,1)}) custom-call(s32[2]{0:T(128)} %seeds_hbm.1, s32[1,16]{1,0:T(1,128)} %count_hbm.1, f32[8,256]{1,0:T(8,128)} %diff_hbm.1, s32[8,256]{1,0:T(8,128)} %wet_hbm.1, f32[75,75]{1,0:T(8,128)} %vert_hbm.1, f32[8,256]{1,0:T(8,128)} %scale_hbm.1, s32[1,16,128]{2,1,0:T(8,128)} %cell_hbm.1, ...), custom_call_target="tpu_custom_call" | custom-call | tf_op jit(solution)/shard_map/pallas_call | solution.py:407
  24.3 0.0 copy-start
  24.3 1.8 %copy.10 = bf16[1,16,75,128]{3,1,2,0:T(8,128)(2,1)} copy(bf16[1,16,75,128]{3,2,1,0:T(8,128)(2,1)} %get-tuple-element.3) | data formatting | bytes 614400 | tf_op jit(solution)/shard_map/pallas_call | solution.py:407
  26.1 0.0 copy-done
  26.1 0.7 %copy.12 = bf16[75,8,256]{2,1,0:T(8,128)(2,1)} copy(bf16[75,8,256]{2,1,0:T(8,128)(2,1)S(1)} %copy-done) | data formatting | bytes 614400
Async XLA Ops:
  24.3 1.8 %copy-start = (bf16[75,8,256]{2,1,0:T(8,128)(2,1)S(1)}, bf16[75,8,256]{2,1,0:T(8,128)(2,1)}, u32[]{:S(2)}) copy-start(bf16[75,8,256]{2,1,0:T(8,128)(2,1)} %get-tuple-element.6) | copy-start | bytes 921604

commit v8 on v6

--- a/solution.py
+++ b/solution.py
@@ -9,6 +9,7 @@
 
 STEPS = 8
 GROUP = 8
+CHUNKS = 4
 SPREAD = 3.4641016151377544
 MESH = pl.DeviceIdType.MESH
 
@@ -60,6 +61,7 @@
     shares,
     field,
     field_rows,
+    prof_rows,
     prof_send,
     prof_recv,
     edge_ss,
@@ -381,8 +383,10 @@
         mixed = mixed[0:padded] + mixed[padded : 2 * padded]
         for side in range(2):
             live = slot_ids < count_ref[0, source + side]
-            mine = mixed[0:levels, side * slots : (side + 1) * slots]
-            prof_ref[0, source + side] = jnp.where(live, mine, 0.0).astype(jnp.bfloat16)
+            prof_rows[:, source + side, :] = jnp.where(
+                live, mixed[:, side * slots : (side + 1) * slots], 0.0
+            )
+    prof_ref[...] = prof_rows[0:levels].astype(jnp.bfloat16)
 
     def settle(k, carry):
         peer = lax.rem(me + k, n)
@@ -393,6 +397,22 @@
     lax.fori_loop(1, n, settle, 0)
     for which in range(3):
         edge_copy(which).wait_send()
+
+
+def hand_over(pert_in, prof_in, pert_out, prof_out, sems):
+    levels = pert_in.shape[0]
+    size = -(-levels // CHUNKS)
+    copies = []
+    for k in range(CHUNKS):
+        part = pl.ds(k * size, min(size, levels - k * size))
+        for source, target in ((pert_in, pert_out), (prof_in, prof_out)):
+            copies.append(
+                pltpu.make_async_copy(source.at[part], target.at[part], sems.at[len(copies)])
+            )
+    for copy in copies:
+        copy.start()
+    for copy in copies:
+        copy.wait()
 
 
 def body(
@@ -411,11 +431,11 @@
     vmem = pl.BlockSpec(memory_space=pltpu.VMEM)
     hbm = pl.BlockSpec(memory_space=pltpu.HBM)
     dma = pltpu.SemaphoreType.DMA
-    return pl.pallas_call(
+    perturbation, profiles = pl.pallas_call(
         functools.partial(kernel, n),
         out_shape=(
             jax.ShapeDtypeStruct((levels, rows, cols), bf16),
-            jax.ShapeDtypeStruct((1, n, levels, slots), bf16),
+            jax.ShapeDtypeStruct((levels, n, slots), bf16),
         ),
         in_specs=[hbm] * 8,
         out_specs=(vmem, vmem),
@@ -449,6 +469,7 @@
             pltpu.VMEM((n // 2, 2 * GROUP, 2 * slots), f32),
             pltpu.VMEM((rows * padded, cols), bf16),
             pltpu.VMEM((padded, rows, cols), f32),
+            pltpu.VMEM((padded, n, slots), f32),
             pltpu.VMEM((n, padded, slots), bf16),
             pltpu.VMEM((n, padded, slots), bf16),
             dma((3,)),
@@ -471,6 +492,18 @@
         obs_cell,
         obs_frac,
     )
+    perturbation, profiles = pl.pallas_call(
+        hand_over,
+        out_shape=(
+            jax.ShapeDtypeStruct(perturbation.shape, bf16),
+            jax.ShapeDtypeStruct(profiles.shape, bf16),
+        ),
+        in_specs=[hbm, hbm],
+        out_specs=(hbm, hbm),
+        scratch_shapes=[dma((2 * CHUNKS,))],
+        compiler_params=pltpu.CompilerParams(vmem_limit_bytes=60 * 1024 * 1024),
+    )(perturbation, profiles)
+    return (perturbation, jnp.transpose(profiles, (1, 0, 2))[None])
 
 
 def solution(mesh):

time: 26.8 us -> 44.3 us (1.65)
  Pallas kernels: 23.4 us -> 43.4 us
  local copies, waits for them, and re-layouts: 2.54 us -> 0 us
    pallas_call x0 -> x1, Pallas kernels: none -> 19.8 us  [body(): pl.pallas_call(hand_over, out_shape=(jax.ShapeDtypeStruct(perturbation.sh...]
    pallas_call x1 -> x0, local copies, waits for them, and re-layouts: 1.81 us -> none  [body(): pl.pallas_call(functools.partial(kernel, n), out_shape=(jax.ShapeDtypeStr...]
    unnamed x3 -> x0, local copies, waits for them, and re-layouts: 0.72 us -> none
where the time goes in v8:
time: 44.3 us; the launch traced here: 44.1 us
  Pallas kernels  43.4 us (98%)
  between operations  0.64 us (1%)
    pallas_call x1, Pallas kernels, body(): pl.pallas_call(functools.partial(kernel, n), out_shape=(jax.ShapeDtypeStr...  23.6 us
    pallas_call x1, Pallas kernels, body(): pl.pallas_call(hand_over, out_shape=(jax.ShapeDtypeStruct(perturbation.sh...  19.8 us

profile of v8, /device:TPU:0, one launch (start us, length us, event | category | flops | bytes accessed | tf_op | source)
XLA Modules:
  0.0 44.1 jit_solution(15969997645551645762)
XLA Ops:
  0.6 23.6 %shard_map.95 = (bf16[75,8,256]{2,1,0:T(8,128)(2,1)}, bf16[75,16,128]{2,1,0:T(8,128)(2,1)}) custom-call(s32[2]{0:T(128)} %seeds_hbm.1, s32[1,16]{1,0:T(1,128)} %count_hbm.1, f32[8,256]{1,0:T(8,128)} %diff_hbm.1, s32[8,256]{1,0:T(8,128)} %wet_hbm.1, f32[75,75]{1,0:T(8,128)} %vert_hbm.1, f32[8,256]{1,0:T(8,128)} %scale_hbm.1, s32[1,16,128]{2,1,0:T(8,128)} %cell_hbm.1, ...), custom_call_target="tpu_custom_call" | custom-call | tf_op jit(solution)/shard_map/pallas_call | solution.py:434
  24.3 19.8 %shard_map.96 = (bf16[75,8,256]{2,1,0:T(8,128)(2,1)}, bf16[75,16,128]{2,1,0:T(8,128)(2,1)}) custom-call(bf16[75,8,256]{2,1,0:T(8,128)(2,1)} %get-tuple-element.6.pert_in, bf16[75,16,128]{2,1,0:T(8,128)(2,1)} %get-tuple-element.7.prof_in), custom_call_target="tpu_custom_call" | custom-call | tf_op jit(solution)/shard_map/pallas_call | solution.py:495
